TPU v7x, 128 devices: a whole 4x4x4 slice. The times are simulated.
128 devices in a mesh: head: 4 (over y), probe: 32 (over z, x, core).
Axes of the slice: x: 4, y: 4, z: 4, core: 2. Of those that a mesh axis runs over, the one named last changes fastest.
Arguments:
- history_keys: bfloat16 [8, 16384, 128], P('head'), may hold values from -4 to 4, as said below
- history_values: bfloat16 [8, 16384, 128], P('head'), as said below
- queries: bfloat16 [8, 16384, 128], P('head', 'probe'), as said below
- positions: int32 [8, 16384], P('head', 'probe'), may hold values from 8192 to 16383
- kept_index: int32 [8, 2048], P('head'), may hold values from 0 to 16383, as said below
Outputs:
- correction: float32 [8, 2048, 128], P('head', 'probe')
Inputs may be any that keep to these rules, and one draw needn't show every extreme that they name: `kept_index`: in each head, slot i holds a history position in [i * 8, (i + 1) * 8); slot 0 holds position 0 and the last slot position 16383. `queries`: probe query vectors of each head. `history_keys`: history keys of each head. `history_values`: history values of each head.
All inputs are finite; a program needn't handle non-finite values.
Results may differ from a plain program's by a relative error of at most 0.0006.
Values sent between devices are 32-bit elements; how exact they have to be, the bound alone decides.
No kernel may reach another device: no remote copies, remote signals or barrier semaphores. Data moves between devices by JAX's collectives and lax.ppermute only.
A program may use at most 128 MiB of HBM per device.

v0:
```python
import math

import jax
import jax.numpy as jnp
from jax import lax
from jax.sharding import PartitionSpec as P

ITERS = 2


HIGH = lax.Precision.HIGHEST


def masked_parts(scores, visible):
    peak = jnp.max(jnp.where(visible, scores, -jnp.inf), axis=-1, keepdims=True)
    expo = jnp.exp(jnp.where(visible, scores - peak, -jnp.inf))
    return (expo, jnp.sum(expo, axis=-1, keepdims=True))


def head_target(keys, values, probe_rows, probe_pos):
    block = min(512, probe_rows.shape[0])
    scale = 1.0 / math.sqrt(probe_rows.shape[1])
    rows_blocks = probe_rows.reshape(-1, block, probe_rows.shape[1])
    pos_blocks = probe_pos.reshape(-1, block)
    order = jnp.arange(keys.shape[0], dtype=jnp.int32)

    def one_block(pieces):
        rows_now, pos_now = pieces
        scores = jnp.dot(rows_now, keys.T, preferred_element_type=jnp.float32) * scale
        visible = order[None, :] <= pos_now[:, None]
        expo, total = masked_parts(scores, visible)
        mixed = jnp.dot(expo.astype(jnp.bfloat16), values, preferred_element_type=jnp.float32)
        return mixed / total

    return lax.map(one_block, (rows_blocks, pos_blocks)).reshape(probe_rows.shape[0], -1)


def local(history_keys, history_values, queries, positions, kept_index):
    kept_count = kept_index.shape[1]
    scale = 1.0 / math.sqrt(queries.shape[2])
    ridge = queries.shape[1] * lax.axis_size("probe") / (kept_count * kept_count)
    own_count = kept_count // lax.axis_size("probe")
    own_first = lax.axis_index("probe") * own_count
    kept_keys = jnp.take_along_axis(history_keys, kept_index[:, :, None], axis=1)
    start_values = jnp.take_along_axis(history_values, kept_index[:, :, None], axis=1).astype(
        jnp.float32
    )
    scores = (
        jnp.einsum("hpd,hkd->hpk", queries, kept_keys, preferred_element_type=jnp.float32) * scale
    )
    visible = kept_index[:, None, :] <= positions[:, :, None]
    expo, total = masked_parts(scores, visible)
    weights = expo / total

    def forward(vec):
        return jnp.einsum(
            "hpk,hkd->hpd", weights, vec, precision=HIGH, preferred_element_type=jnp.float32
        )

    def backward(image):
        return jnp.einsum(
            "hpk,hpd->hkd", weights, image, precision=HIGH, preferred_element_type=jnp.float32
        )

    def total_terms(term):
        return lax.psum(term, "probe")

    def global_dot(left, right):
        return lax.psum(jnp.sum(left * right), "head")

    targets = lax.map(
        lambda pieces: head_target(*pieces), (history_keys, history_values, queries, positions)
    )
    residual = total_terms(backward(targets - forward(start_values)))
    direction = residual
    norm_now = global_dot(residual, residual)
    correction = jnp.zeros_like(residual)
    for step in range(ITERS):
        image = total_terms(backward(forward(direction))) + ridge * direction
        alpha = norm_now / global_dot(direction, image)
        correction = correction + alpha * direction
        if step + 1 < ITERS:
            residual = residual - alpha * image
            norm_next = global_dot(residual, residual)
            direction = residual + norm_next / norm_now * direction
            norm_now = norm_next
    return lax.dynamic_slice_in_dim(correction, own_first, own_count, 1)


def solution(mesh):
    return jax.shard_map(
        local,
        mesh=mesh,
        in_specs=(
            P("head", None, None),
            P("head", None, None),
            P("head", "probe", None),
            P("head", "probe"),
            P("head", None),
        ),
        out_specs=P("head", "probe", None),
        check_vma=False,
    )
```

profile of v0, /device:TPU:1, one launch (start us, length us, event | category | flops | bytes accessed | tf_op | source)
XLA Modules:
  0.0 693.9 jit_solution(16680355917840956667)
XLA Ops:
  6.5 0.0 all-reduce.5.cloned.1.call-start
  6.5 0.7 or_bitcast_fusion
  7.3 1.3 and_bitcast_fusion
  8.6 69.7 %gather_fusion.1 = bf16[4096,128]{1,0:T(8,128)(2,1)} fusion(bf16[2,16384,128]{2,1,0:T(8,128)(2,1)} %param.10, s32[4096]{0:T(1024)S(1)} %bitcast.67), kind=kCustom, calls=%fused_computation.1.clone | custom fusion | bytes 2129920 | tf_op jit(solution)/shard_map/jit(take_along_axis)/gather | solution.py:45
  78.3 69.7 %gather_fusion = bf16[4096,128]{1,0:T(8,128)(2,1)} fusion(bf16[2,16384,128]{2,1,0:T(8,128)(2,1)} %param.9, s32[4096]{0:T(1024)S(1)} %bitcast.68), kind=kCustom, calls=%fused_computation.clone | custom fusion | bytes 2129920 | tf_op jit(solution)/shard_map/jit(take_along_axis)/gather | solution.py:44
  148.0 0.0 copy-done.4
  148.0 0.0 copy-done.7
  148.0 0.0 copy-start.5
  148.0 96.3 %while.10 = (s32[]{:T(128)}, f32[2,512,128]{2,1,0:T(8,128)S(1)}, s32[2,512]{1,0:T(2,128)S(1)}, bf16[2,512,128]{2,1,0:T(8,128)(2,1)S(1)}, bf16[2,16384,128]{2,1,0...) while((s32[]{:T(128)}, f32[2,512,128]{2,1,0:T(8,128)S(1)}, s32[2,512]{1,0:T(2,128)S(1)}, ...), condition=%wide.region_5.7_spmd, body=%wide.region_2.6_spmd.sunk | while | flops 4412472320 | bytes 109467736 | solution.py:71
  148.1 16.0 %select_reduce_fusion.2 = (f32[512]{0:T(512)S(1)}, f32[512,16384]{1,0:T(8,128)}) fusion(s32[512]{0:T(512)S(1)} %bitcast.71, bf16[2,16384,128]{2,1,0:T(8,128)(2,1)} %get-tuple-element.139, s32[]{:T(128)S(6)} %copy.10, bf16[2,512,128]{2,1,0:T(8,128)(2,1)S(1)} %get-tuple-element.138), kind=kOutput, calls=%fused_computation.3.clone.1 | convolution fusion | flops 2181037568 | bytes 37884928 | tf_op jit(solution)/shard_map/while/body/eval_jaxpr/while/body/eval_jaxpr/dot_general | solution.py:29
  164.1 15.5 %fusion.67 = f32[512]{0:T(512)S(1)} fusion(f32[512,16384]{1,0:T(8,128)} %get-tuple-element.119, f32[512]{0:T(512)S(1)} %get-tuple-element.120, s32[512]{0:T(512)S(1)} %bitcast.72), kind=kLoop, calls=%fused_computation.5.clone.1 | loop fusion | flops 41942528 | bytes 33560576 | tf_op jit(solution)/shard_map/while/body/eval_jaxpr/while/body/eval_jaxpr/reduce_sum | solution.py:17
  179.6 16.6 %fusion.68 = f32[2,512,128]{2,1,0:T(8,128)S(1)} fusion(f32[2,512,128]{2,1,0:T(8,128)S(1)} %get-tuple-element.129, s32[]{:T(128)S(6)} %copy.10, bf16[2,16384,128]{2,1,0:T(8,128)(2,1)} %get-tuple-element.140, f32[512,16384]{1,0:T(8,128)} %get-tuple-element.119, f32[512]{0:T(512)S(1)} %get-tuple-element.120, s32[512]{0:T(512)S(1)} %bitcast.73, ...), kind=kOutput, calls=%fused_computation.15.clone.1 | convolution fusion | flops 2189492224 | bytes 38018048 | tf_op jit(solution)/shard_map/while/body/eval_jaxpr/while/body/eval_jaxpr/dot_general | solution.py:32
  196.2 15.9 %select_reduce_fusion.2 = (f32[512]{0:T(512)S(1)}, f32[512,16384]{1,0:T(8,128)}) fusion(s32[512]{0:T(512)S(1)} %bitcast.71, bf16[2,16384,128]{2,1,0:T(8,128)(2,1)} %get-tuple-element.139, s32[]{:T(128)S(6)} %copy.10, bf16[2,512,128]{2,1,0:T(8,128)(2,1)S(1)} %get-tuple-element.138), kind=kOutput, calls=%fused_computation.3.clone.1 | convolution fusion | flops 2181037568 | bytes 37884928 | tf_op jit(solution)/shard_map/while/body/eval_jaxpr/while/body/eval_jaxpr/dot_general | solution.py:29
  212.2 15.5 %fusion.67 = f32[512]{0:T(512)S(1)} fusion(f32[512,16384]{1,0:T(8,128)} %get-tuple-element.119, f32[512]{0:T(512)S(1)} %get-tuple-element.120, s32[512]{0:T(512)S(1)} %bitcast.72), kind=kLoop, calls=%fused_computation.5.clone.1 | loop fusion | flops 41942528 | bytes 33560576 | tf_op jit(solution)/shard_map/while/body/eval_jaxpr/while/body/eval_jaxpr/reduce_sum | solution.py:17
  227.7 16.6 %fusion.68 = f32[2,512,128]{2,1,0:T(8,128)S(1)} fusion(f32[2,512,128]{2,1,0:T(8,128)S(1)} %get-tuple-element.129, s32[]{:T(128)S(6)} %copy.10, bf16[2,16384,128]{2,1,0:T(8,128)(2,1)} %get-tuple-element.140, f32[512,16384]{1,0:T(8,128)} %get-tuple-element.119, f32[512]{0:T(512)S(1)} %get-tuple-element.120, s32[512]{0:T(512)S(1)} %bitcast.73, ...), kind=kOutput, calls=%fused_computation.15.clone.1 | convolution fusion | flops 2189492224 | bytes 38018048 | tf_op jit(solution)/shard_map/while/body/eval_jaxpr/while/body/eval_jaxpr/dot_general | solution.py:32
  244.3 0.0 copy-start.6
  244.3 0.0 copy-done.2
  244.3 0.0 copy-done.5
  244.3 2.0 fusion.38
  246.4 0.0 copy-done.6
  246.4 0.0 copy-start.3
  246.4 3.5 fusion.54
  249.9 0.0 copy-start.8
  249.9 7.5 %convolution_subtract_fusion = f32[2,512,128]{2,1,0:T(8,128)S(1)} fusion(f32[2,512,128]{2,1,0:T(8,128)S(1)} %get-tuple-element.59, bf16[2,2048,128]{2,1,0:T(8,128)(2,1)S(1)} %bitcast.70, pred[2,2048]{1,0:T(4,128)(4,1)S(1)} %copy-done.5, f32[2,512,2048]{1,2,0:T(8,128)S(1)} %get-tuple-element.79, f32[2,512]{1,0:T(2,128)S(1)} %get-tuple-element.78), kind=kOutput, calls=%fused_computation.41 | convolution fusion | flops 3223977984 | bytes 10493952 | tf_op jit(solution)/shard_map/hpk,hkd->hpd/dot_general | solution.py:56
  257.4 0.0 copy-done.8
  257.5 8.8 %fusion.53 = f32[2,2048,128]{2,1,0:T(8,128)} fusion(f32[2,512,128]{2,1,0:T(8,128)S(1)} %convolution_subtract_fusion, f32[2,512,2048]{1,2,0:T(8,128)S(1)} %get-tuple-element.79, f32[2,512]{1,0:T(2,128)S(1)} %get-tuple-element.78), kind=kOutput, calls=%fused_computation.63 | convolution fusion | flops 3223322624 | bytes 11014144 | tf_op jit(solution)/shard_map/hpk,hpd->hkd/dot_general | solution.py:61
  266.3 0.0 all-reduce.5.cloned.1.call-update
  266.3 0.0 all-reduce.7.cloned.1.call-start
  266.3 110.8 %all-reduce.5.cloned.1.call-done = f32[2,2048,128]{2,1,0:T(8,128)} async-done(((f32[2,2048,128]{2,1,0:T(8,128)}), f32[2,2048,128]{2,1,0:T(8,128)}) %all-reduce.5.cloned.1.call-update) | async-done | bytes 2097168 | tf_op jit(solution)/shard_map/psum | solution.py:66
  377.1 16.0 %fusion.52 = f32[2,512,128]{2,1,0:T(8,128)S(1)} fusion(f32[2,2048,128]{2,1,0:T(8,128)} %all-reduce.5.cloned.1.call-done, f32[2,512,2048]{1,2,0:T(8,128)} %copy-done.8, f32[2,512]{1,0:T(2,128)S(1)} %get-tuple-element.78), kind=kOutput, calls=%fused_computation.62 | convolution fusion | flops 3223322624 | bytes 11014144 | tf_op jit(solution)/shard_map/hpk,hkd->hpd/dot_general | solution.py:56
  393.1 10.2 %fusion.51 = f32[2,2048,128]{2,1,0:T(8,128)} fusion(f32[2,512,128]{2,1,0:T(8,128)S(1)} %fusion.52, f32[2,512,2048]{1,2,0:T(8,128)} %copy-done.8, f32[2,512]{1,0:T(2,128)S(1)} %get-tuple-element.78), kind=kOutput, calls=%fused_computation.61 | convolution fusion | flops 3223322624 | bytes 11014144 | tf_op jit(solution)/shard_map/hpk,hpd->hkd/dot_general | solution.py:61
  403.4 0.0 all-reduce.7.cloned.1.call-update
  403.4 0.0 all-reduce.9.cloned.1.call-start
  403.4 107.2 %all-reduce.7.cloned.1.call-done = f32[2,2048,128]{2,1,0:T(8,128)} async-done(((f32[2,2048,128]{2,1,0:T(8,128)}), f32[2,2048,128]{2,1,0:T(8,128)}) %all-reduce.7.cloned.1.call-update) | async-done | bytes 2097168 | tf_op jit(solution)/shard_map/psum | solution.py:66
  510.6 2.8 multiply_reduce_fusion.2
  513.4 9.1 %all-reduce = (f32[]{:T(128)}, f32[]{:T(128)}) all-reduce(f32[]{:T(128)} %get-tuple-element.61, f32[]{:T(128)} %get-tuple-element.60), channel_id=1, replica_groups=mesh['head'=4,'probe'=32] {'head'}, use_global_device_ids=true, to_apply=%region_8.10 | all-reduce | flops 2 | bytes 16 | tf_op jit(solution)/shard_map/psum | solution.py:69
  523.7 2.7 multiply_reduce_fusion.1
  526.5 6.8 psum.53
  534.5 0.0 slice-start
  534.5 2.2 multiply_add_fusion
  536.7 0.0 slice-start.1
  536.7 16.6 %fusion.50 = f32[2,512,128]{2,1,0:T(8,128)S(1)} fusion(f32[2,2048,128]{2,1,0:T(8,128)S(1)} %multiply_add_fusion, f32[2,512,2048]{1,2,0:T(8,128)} %copy-done.8, f32[2,512]{1,0:T(2,128)S(1)} %get-tuple-element.78), kind=kOutput, calls=%fused_computation.60 | convolution fusion | flops 3223322624 | bytes 11014144 | tf_op jit(solution)/shard_map/hpk,hkd->hpd/dot_general | solution.py:56
  553.4 8.7 %fusion.49 = f32[2,2048,128]{2,1,0:T(8,128)} fusion(f32[2,512,128]{2,1,0:T(8,128)S(1)} %fusion.50, f32[2,512,2048]{1,2,0:T(8,128)S(1)} %bitcast.75, f32[2,512]{1,0:T(2,128)S(1)} %get-tuple-element.78), kind=kOutput, calls=%fused_computation.59 | convolution fusion | flops 3223322624 | bytes 11014144 | tf_op jit(solution)/shard_map/hpk,hpd->hkd/dot_general | solution.py:61
  562.0 0.0 all-reduce.9.cloned.1.call-update
  562.1 109.6 %all-reduce.9.cloned.1.call-done = f32[2,2048,128]{2,1,0:T(8,128)} async-done(((f32[2,2048,128]{2,1,0:T(8,128)}), f32[2,2048,128]{2,1,0:T(8,128)}) %all-reduce.9.cloned.1.call-update) | async-done | bytes 2097168 | tf_op jit(solution)/shard_map/psum | solution.py:66
  671.7 3.4 multiply_reduce_fusion
  675.0 9.1 %psum.55 = f32[]{:T(128)} all-reduce(f32[]{:T(128)} %multiply_reduce_fusion), channel_id=1, replica_groups=mesh['head'=4,'probe'=32] {'head'}, use_global_device_ids=true, to_apply=%region_16.18 | all-reduce | flops 1 | bytes 8 | tf_op jit(solution)/shard_map/psum | solution.py:69
  685.4 1.5 fusion.44
  (15 shorter events, 0.0 us)
Async XLA Ops:
  6.5 370.6 %all-reduce.5.cloned.1.call-start = ((), (), s32[]{:S(2)}) async-start(), calls=%async_computation | async-start | bytes 4194304 | tf_op jit(solution)/shard_map/psum | solution.py:66
  78.3 69.7 %copy-start.4 = (bf16[2,512,128]{2,1,0:T(8,128)(2,1)S(1)}, bf16[2,512,128]{2,1,0:T(8,128)(2,1)}, u32[]{:S(2)}) copy-start(bf16[2,512,128]{2,1,0:T(8,128)(2,1)} %param.11) | copy-start | bytes 786436
  78.3 69.7 %copy-start.7 = (s32[2,512]{1,0:T(2,128)S(1)}, s32[2,512]{1,0:T(2,128)}, u32[]{:S(2)}) copy-start(s32[2,512]{1,0:T(2,128)} %param.12) | copy-start | bytes 12292
  148.0 96.3 %copy-start.2 = (bf16[4096,128]{1,0:T(8,128)(2,1)S(1)}, bf16[4096,128]{1,0:T(8,128)(2,1)}, u32[]{:S(2)}) copy-start(bf16[4096,128]{1,0:T(8,128)(2,1)} %gather_fusion) | copy-start | bytes 3145732
  148.0 96.3 %copy-start.5 = (pred[2,2048]{1,0:T(4,128)(4,1)S(1)}, pred[2,2048]{1,0:T(4,128)(4,1)}, u32[]{:S(2)}) copy-start(pred[2,2048]{1,0:T(4,128)(4,1)} %and_bitcast_fusion) | copy-start | bytes 12292
  244.3 2.0 copy-start.6
  246.4 3.6 copy-start.3
  249.9 7.5 %copy-start.8 = (f32[2,512,2048]{1,2,0:T(8,128)}, f32[2,512,2048]{1,2,0:T(8,128)S(1)}, u32[]{:S(2)}) copy-start(f32[2,512,2048]{1,2,0:T(8,128)S(1)} %get-tuple-element.79) | copy-start | bytes 25165828
  266.3 244.3 %all-reduce.7.cloned.1.call-start = ((), (), s32[]{:S(2)}) async-start(), calls=%async_computation.1 | async-start | bytes 4194304 | tf_op jit(solution)/shard_map/psum | solution.py:66
  393.1 117.5 %copy-start = (f32[2,2048,128]{2,1,0:T(8,128)S(1)}, f32[2,2048,128]{2,1,0:T(8,128)}, u32[]{:S(2)}) copy-start(f32[2,2048,128]{2,1,0:T(8,128)} %all-reduce.5.cloned.1.call-done) | copy-start | bytes 6291460
  403.4 268.3 %all-reduce.9.cloned.1.call-start = ((), (), s32[]{:S(2)}) async-start(), calls=%async_computation.2 | async-start | bytes 4194304 | tf_op jit(solution)/shard_map/psum | solution.py:66
  534.5 18.8 %slice-start = ((s8[8388608]{0:T(1024)(128)(4,1)}), s8[4194304]{0:T(1024)(128)(4,1)S(1)}, s32[]{:S(2)}) async-start(s8[8388608]{0:T(1024)(128)(4,1)} %bitcast.74), calls=%async_computation.3 | async-start | bytes 8388608
  536.7 16.6 %copy-start.1 = (f32[2,2048,128]{2,1,0:T(8,128)}, f32[2,2048,128]{2,1,0:T(8,128)S(1)}, u32[]{:S(2)}) copy-start(f32[2,2048,128]{2,1,0:T(8,128)S(1)} %multiply_add_fusion) | copy-start | bytes 6291460
  536.7 16.6 %slice-start.1 = ((s8[8388608]{0:T(1024)(128)(4,1)}), s8[4194304]{0:T(1024)(128)(4,1)S(1)}, s32[]{:S(2)}) async-start(s8[8388608]{0:T(1024)(128)(4,1)} %bitcast.74), calls=%async_computation.4 | async-start | bytes 8388608
Sparse Core Ops, SparseCore 0:
  266.4 110.6 all-reduce.4
  403.5 107.0 all-reduce.6
  562.2 109.4 all-reduce.8
where the time goes:
time: 706 us; the launch traced here: 694 us
  waiting for transfers between devices  328 us (46%)
  local copies, waits for them, and re-layouts  139 us (20%)
  matrix products  135 us (19%)
  other arithmetic  49.2 us (7%)
  blocking collectives  24.9 us (4%)
  between operations  17.5 us (2%)
    psum x3, waiting for transfers between devices, total_terms(): return lax.psum(term, 'probe')  328 us
    gather x1, local copies, waits for them, and re-layouts, local(): jnp.take_along_axis(history_keys, kept_index[:, :, None], axis=1)  69.7 us
    gather x1, local copies, waits for them, and re-layouts, local(): jnp.take_along_axis(history_values, kept_index[:, :, None], axis=1)  69.7 us
    dot_general x3, matrix products, forward(): jnp.einsum('hpk,hkd->hpd', weights, vec, precision=HIGH, preferred_elemen...  40.1 us
    dot_general x2, matrix products, one_block(): jnp.dot(expo.astype(jnp.bfloat16), values, preferred_element_type=jnp.flo...  33.2 us
    dot_general x2, matrix products, one_block(): jnp.dot(rows_now, keys.T, preferred_element_type=jnp.float32) * scale  32 us
    reduce_sum x2, other arithmetic, masked_parts(): return (expo, jnp.sum(expo, axis=-1, keepdims=True))  31.1 us
    dot_general x3, matrix products, backward(): jnp.einsum('hpk,hpd->hkd', weights, image, precision=HIGH, preferred_elem...  27.7 us
  transfers between devices with their start and end apart: 3, of which 3 were waited for; matrix products, arithmetic and copies ran while one was open for 0% of the time, Pallas kernels for 0%

commit v1 on v0

v1 whole, which is shorter than its diff:
```python
import functools
import math

import jax
import jax.numpy as jnp
from jax import lax
from jax.experimental import pallas as pl
from jax.experimental.pallas import tpu as pltpu
from jax.sharding import PartitionSpec as P

HD = 128
BLOCK = 2048
ROWS = 256
MIB = 1024 * 1024
f32 = jnp.float32
bf16 = jnp.bfloat16
NT = (((1,), (1,)), ((), ()))
NN = (((1,), (0,)), ((), ()))


def dot(left, right, dims=NN):
    return lax.dot_general(left, right, dims, preferred_element_type=f32)


def halves(wide):
    high = wide.astype(bf16)
    return high, (wide - high.astype(f32)).astype(bf16)


def column(ref, tile):
    return jnp.transpose(ref[...])[:, tile : tile + 1]


def attend_kernel(core, q_ref, pos_ref, kept_ref, k_ref, v_ref, t_ref, q2_ref, kk_ref, kv_ref, m_ref, acc_ref, k2_ref, v2_ref):
    step = pl.program_id(0)
    rows = q_ref.shape[0]
    tiles = rows // ROWS
    per = BLOCK // 8

    @pl.when(step == 0)
    def _():
        high, low = halves(q_ref[...])
        q2_ref[:, :HD] = high
        q2_ref[:, HD:] = low
        m_ref[...] = jnp.full(m_ref.shape, -jnp.inf, f32)
        acc_ref[...] = jnp.zeros(acc_ref.shape, f32)
        v2_ref[:, HD:] = jnp.ones((BLOCK, HD), bf16)

    keys = k_ref[0]
    values = v_ref[0]
    k2_ref[:, :HD] = keys
    k2_ref[:, HD:] = keys
    v2_ref[:, :HD] = values

    part = 1024
    slots = part // 8
    kept_cols = jnp.transpose(kept_ref[...])
    for piece in range(BLOCK // part):
        lane = lax.broadcasted_iota(jnp.int32, (slots, part), 1)
        want = kept_cols[:, piece : piece + 1] - (step * BLOCK + piece * part)
        hot = jnp.where(lane == want, 1.0, 0.0).astype(bf16)
        both = jnp.concatenate([k_ref[0, pl.ds(piece * part, part), :], v_ref[0, pl.ds(piece * part, part), :]], axis=1)
        got = dot(hot, both)
        kk_ref[pl.ds(piece * slots, slots), :] = got[:, :HD].astype(bf16)
        kv_ref[pl.ds(piece * slots, slots), :] = got[:, HD:].astype(bf16)

    def go(masked):
        pos_cols = jnp.transpose(pos_ref[...]).astype(jnp.int32) - step * BLOCK
        for tile in range(tiles):
            here = pl.ds(tile * ROWS, ROWS)
            scores = dot(q2_ref[here, :], k2_ref[...], NT)
            if masked:
                pos = jnp.concatenate(
                    [pos_cols[:, i : i + 1] for i in range(tile * ROWS // 128, (tile + 1) * ROWS // 128)], axis=0
                )
                lane = lax.broadcasted_iota(jnp.int32, scores.shape, 1)
                scores = jnp.where(lane <= pos, scores, -jnp.inf)
            old = m_ref[here, :]
            new = jnp.maximum(old, jnp.max(scores, axis=1, keepdims=True))
            m_ref[here, :] = new
            expo = jnp.exp2(scores - new[:, :1]).astype(bf16)
            fade = jnp.exp2(old - new)
            fade2 = jnp.concatenate([fade, fade], axis=1)
            acc_ref[here, :] = acc_ref[here, :] * fade2 + dot(expo, v2_ref[...])

    half = pl.num_programs(0) // 2

    @pl.when(step < half)
    def _():
        go(False)

    @pl.when(step >= half)
    def _():
        go(True)

    @pl.when(step == pl.num_programs(0) - 1)
    def _():
        t_ref[...] = acc_ref[:, :HD] / acc_ref[:, HD:]


def attend(core, q, pos, kept, keys, values):
    rows = q.shape[0]
    hist = keys.shape[1]
    steps = hist // BLOCK
    per = BLOCK // 8
    kept_count = kept.shape[0] * kept.shape[1]
    whole = lambda shape: pl.BlockSpec(shape, lambda j, c: (0,) * len(shape))
    return pl.pallas_call(
        attend_kernel,
        grid_spec=pltpu.PrefetchScalarGridSpec(
            num_scalar_prefetch=1,
            grid=(steps,),
            in_specs=[
                whole((rows, HD)),
                whole(pos.shape),
                pl.BlockSpec((None, per // 128, 128), lambda j, c: (j, 0, 0)),
                pl.BlockSpec((1, BLOCK, HD), lambda j, c: (c[0], j, 0)),
                pl.BlockSpec((1, BLOCK, HD), lambda j, c: (c[0], j, 0)),
            ],
            out_specs=[
                whole((rows, HD)),
                whole((rows, 2 * HD)),
                pl.BlockSpec((per, HD), lambda j, c: (j, 0)),
                pl.BlockSpec((per, HD), lambda j, c: (j, 0)),
            ],
            scratch_shapes=[
                pltpu.VMEM((rows, HD), f32),
                pltpu.VMEM((rows, 2 * HD), f32),
                pltpu.VMEM((BLOCK, 2 * HD), bf16),
                pltpu.VMEM((BLOCK, 2 * HD), bf16),
            ],
        ),
        out_shape=[
            jax.ShapeDtypeStruct((rows, HD), f32),
            jax.ShapeDtypeStruct((rows, 2 * HD), bf16),
            jax.ShapeDtypeStruct((kept_count, HD), bf16),
            jax.ShapeDtypeStruct((kept_count, HD), bf16),
        ],
        compiler_params=pltpu.CompilerParams(vmem_limit_bytes=40 * MIB),
        name="attend",
    )(core, q, pos, kept.reshape(steps, per // 128, 128), keys, values)


def pull_back(gap_t, wh, wl, z_ref, first):
    high, low = halves(gap_t)
    two = dot(jnp.concatenate([high, low], axis=0), wh)
    part = two[:HD] + two[HD:] + dot(high, wl)
    for chunk in range(z_ref.shape[0]):
        cut = part[:, chunk * 128 : (chunk + 1) * 128]

        @pl.when(first)
        def _():
            z_ref[chunk] = cut

        @pl.when(jnp.logical_not(first))
        def _():
            z_ref[chunk] += cut


def start_kernel(q2_ref, pos_ref, kept_ref, kk_ref, kv_ref, t_ref, wh_ref, wl_ref, z_ref, k2_ref):
    tile = pl.program_id(0)

    @pl.when(tile == 0)
    def _():
        k2_ref[:, :HD] = kk_ref[...]
        k2_ref[:, HD:] = kk_ref[...]

    scores = dot(q2_ref[...], k2_ref[...], NT)
    pos_cols = jnp.transpose(pos_ref[...]).astype(jnp.int32)
    pos = jnp.concatenate([pos_cols[:, i : i + 1] for i in range(ROWS // 128)], axis=0)
    scores = jnp.where(kept_ref[...] <= pos, scores, -jnp.inf)
    expo = jnp.exp2(scores - jnp.max(scores, axis=1, keepdims=True))
    weights = expo * (1.0 / jnp.sum(expo, axis=1, keepdims=True))
    wh, wl = halves(weights)
    wh_ref[...] = wh
    wl_ref[...] = wl
    gap = t_ref[...] - (dot(wh, kv_ref[...]) + dot(wl, kv_ref[...]))
    pull_back(jnp.transpose(gap), wh, wl, z_ref, tile == 0)


def start(q2, pos, kept, kept_keys, kept_values, target):
    rows = q2.shape[0]
    count = kept_keys.shape[0]
    whole = lambda shape: pl.BlockSpec(shape, lambda i: (0,) * len(shape))
    return pl.pallas_call(
        start_kernel,
        grid=(rows // ROWS,),
        in_specs=[
            pl.BlockSpec((ROWS, 2 * HD), lambda i: (i, 0)),
            pl.BlockSpec((None, ROWS // 128, 128), lambda i: (i, 0, 0)),
            whole((1, count)),
            whole((count, HD)),
            whole((count, HD)),
            pl.BlockSpec((ROWS, HD), lambda i: (i, 0)),
        ],
        out_specs=[
            pl.BlockSpec((ROWS, count), lambda i: (i, 0)),
            pl.BlockSpec((ROWS, count), lambda i: (i, 0)),
            whole((count // 128, HD, 128)),
        ],
        out_shape=[
            jax.ShapeDtypeStruct((rows, count), bf16),
            jax.ShapeDtypeStruct((rows, count), bf16),
            jax.ShapeDtypeStruct((count // 128, HD, 128), f32),
        ],
        scratch_shapes=[pltpu.VMEM((count, 2 * HD), bf16)],
        compiler_params=pltpu.CompilerParams(vmem_limit_bytes=40 * MIB),
        name="start",
    )(q2, pos.reshape(rows // ROWS, ROWS // 128, 128), kept.reshape(1, count), kept_keys, kept_values, target)


def load_vector(vec_ref, two_ref):
    for chunk in range(vec_ref.shape[0]):
        high, low = halves(vec_ref[chunk])
        two_ref[:HD, pl.ds(chunk * 128, 128)] = high
        two_ref[HD:, pl.ds(chunk * 128, 128)] = low


def push(two_ref, wh, wl):
    two = dot(two_ref[...], wh, NT)
    return two[:HD] + two[HD:] + dot(two_ref[:HD, :], wl, NT)


def normal_kernel(vec_ref, wh_ref, wl_ref, z_ref, two_ref):
    tile = pl.program_id(0)

    @pl.when(tile == 0)
    def _():
        load_vector(vec_ref, two_ref)

    wh = wh_ref[...]
    wl = wl_ref[...]
    pull_back(push(two_ref, wh, wl), wh, wl, z_ref, tile == 0)


def square_kernel(vec_ref, wh_ref, wl_ref, s_ref, two_ref):
    tile = pl.program_id(0)

    @pl.when(tile == 0)
    def _():
        load_vector(vec_ref, two_ref)
        s_ref[...] = jnp.zeros(s_ref.shape, f32)

    image = push(two_ref, wh_ref[...], wl_ref[...])
    s_ref[...] += jnp.sum(image * image, axis=0, keepdims=True)


def with_weights(kernel, name, out, vec, wh, wl):
    rows, count = wh.shape
    whole = lambda shape: pl.BlockSpec(shape, lambda i: (0,) * len(shape))
    return pl.pallas_call(
        kernel,
        grid=(rows // ROWS,),
        in_specs=[
            whole(vec.shape),
            pl.BlockSpec((ROWS, count), lambda i: (i, 0)),
            pl.BlockSpec((ROWS, count), lambda i: (i, 0)),
        ],
        out_specs=whole(out),
        out_shape=jax.ShapeDtypeStruct(out, f32),
        scratch_shapes=[pltpu.VMEM((2 * HD, count), bf16)],
        compiler_params=pltpu.CompilerParams(vmem_limit_bytes=40 * MIB),
        name=name,
    )(vec, wh, wl)


def local(history_keys, history_values, queries, positions, kept_index):
    count = kept_index.shape[1]
    own_rows = queries.shape[1]
    devices = lax.axis_size("probe")
    chips = devices // 2
    heads = lax.axis_size("head")
    ridge = own_rows * devices / (count * count)
    core = lax.rem(lax.axis_index("probe"), 2)
    swap = [(i, i ^ 1) for i in range(devices)]
    groups = [[2 * i + c for i in range(chips)] for c in range(2)]

    scaled = queries.astype(f32) * (math.log2(math.e) / math.sqrt(HD))
    packed = jnp.concatenate([scaled, positions.astype(f32).reshape(2, own_rows // 128, 128)], axis=1)
    mine = lax.dynamic_index_in_dim(packed, core, 0, keepdims=False)
    other = lax.ppermute(lax.dynamic_index_in_dim(packed, 1 - core, 0, keepdims=False), "probe", swap)
    q = jnp.concatenate([mine[:own_rows], other[:own_rows]], axis=0)
    pos = jnp.concatenate([mine[own_rows:], other[own_rows:]], axis=0)
    kept = lax.dynamic_index_in_dim(kept_index, core, 0, keepdims=False)

    target, q2, kept_keys, kept_values = attend(
        core.astype(jnp.int32).reshape(1), q, pos, kept.reshape(-1, 128), history_keys, history_values
    )
    wh, wl, z = start(q2, pos, kept, kept_keys, kept_values, target)

    def exchange(chunks):
        return lax.all_to_all(chunks, "probe", 0, 0, axis_index_groups=groups, tiled=True)

    def spread(chunk):
        return exchange(jnp.broadcast_to(chunk[None], (chips,) + chunk.shape))

    res = jnp.sum(exchange(z), axis=0)
    z = with_weights(normal_kernel, "normal", z.shape, spread(res), wh, wl)
    image = jnp.sum(exchange(z), axis=0) + ridge * res

    basis = jnp.transpose(jnp.stack([res, image]), (0, 2, 1))
    half = basis.shape[1] // 2
    kept_half = lax.dynamic_slice_in_dim(basis, core * half, half, 1)
    sent_half = lax.dynamic_slice_in_dim(basis, (1 - core) * half, half, 1)
    got_half = lax.ppermute(sent_half, "probe", swap)
    first = jnp.where(core == 0, kept_half, got_half)
    second = jnp.where(core == 0, got_half, kept_half)

    squares = with_weights(square_kernel, "square", (1, ROWS), spread(image), wh, wl)
    sums = jnp.stack([jnp.sum(res * res), jnp.sum(res * image), jnp.sum(image * image), jnp.sum(squares)])
    sums = jnp.broadcast_to(jnp.pad(sums, (0, 124))[None, None], (heads * devices, 1, 128))
    sums = jnp.sum(lax.all_to_all(sums, ("head", "probe"), 0, 0, tiled=True), axis=(0, 1))
    rr, rn, nn, ww = sums[0], sums[1], sums[2], sums[3]
    alpha = rr / rn
    new = rr - 2.0 * alpha * rn + alpha * alpha * nn
    beta = new / rr
    grow = 1.0 + beta
    curve = grow * grow * rn - 2.0 * alpha * grow * nn + alpha * alpha * (ww + ridge * nn)
    step = new / curve
    left = alpha + step * grow
    right = -step * alpha
    return jnp.stack([left * first[0] + right * first[1], left * second[0] + right * second[1]])


def solution(mesh):
    return jax.shard_map(
        local,
        mesh=mesh,
        in_specs=(
            P("head", None, None),
            P("head", None, None),
            P("head", "probe", None),
            P("head", "probe"),
            P("head", None),
        ),
        out_specs=P("head", "probe", None),
        check_vma=False,
    )
```

time: 706 us -> 191 us (0.27); the launches traced: 694 us -> 191 us
  waiting for transfers between devices: 328 us -> 21.5 us
  matrix products: 135 us -> 0 us
  local copies, waits for them, and re-layouts: 139 us -> 19.4 us
  Pallas kernels: 0 us -> 57.9 us
  other arithmetic: 49.2 us -> 6.21 us
  blocking collectives: 24.9 us -> 61.4 us
  starting transfers between devices: 0.09 us -> 17.8 us
  between operations: 17.5 us -> 6.44 us
    psum x3 -> x0, waiting for transfers between devices: 328 us -> none  [total_terms(): return lax.psum(term, 'probe')]
    gather x2 -> x0, local copies, waits for them, and re-layouts: 139 us -> none  [the longest x1 69.7 us: local(): jnp.take_along_axis(history_keys, kept_index[:, :, None], axis=1)]
    dot_general x11 -> x0, matrix products: 135 us -> none  [the longest x3 40.1 us: forward(): jnp.einsum('hpk,hkd->hpd', weights, vec, precision=HIGH, preferred_elemen...]
    all_to_all x0 -> x3, blocking collectives: none -> 61.4 us  [exchange(): lax.all_to_all(chunks, 'probe', 0, 0, axis_index_groups=groups, tiled=True)]
    pallas_call x0 -> x4, Pallas kernels: none -> 57.9 us  [the longest x1 35.3 us: attend(): pl.pallas_call(attend_kernel, grid_spec=pltpu.PrefetchScalarGridSpec(num_...]
    reduce_sum x5, other arithmetic: 40 us -> 1.45 us  [the longest x1 0.7 us: local(): jnp.sum(res * res)]
    psum x3 -> x0, blocking collectives: 24.9 us -> none  [global_dot(): return lax.psum(jnp.sum(left * right), 'head')]
    all_to_all x0 -> x2, waiting for transfers between devices: none -> 20.4 us  [the longest x1 11.1 us: exchange(): lax.all_to_all(chunks, 'probe', 0, 0, axis_index_groups=groups, tiled=True)]
  transfers between devices with their start and end apart: 3 -> 4, of which waited for: 3 -> 3; matrix products, arithmetic and copies ran while one was open for 0% -> 2% of each run, Pallas kernels for 0% -> 2%
where the time goes in v1:
time: 191 us
  blocking collectives  61.4 us (32%)
  Pallas kernels  57.9 us (30%)
  waiting for transfers between devices  21.5 us (11%)
  local copies, waits for them, and re-layouts  19.4 us (10%)
  starting transfers between devices  17.8 us (9%)
  between operations  6.44 us (3%)
  other arithmetic  6.21 us (3%)
    all_to_all x3, blocking collectives, exchange(): lax.all_to_all(chunks, 'probe', 0, 0, axis_index_groups=groups, tiled=True)  61.4 us
    pallas_call x1, Pallas kernels, attend(): pl.pallas_call(attend_kernel, grid_spec=pltpu.PrefetchScalarGridSpec(num_...  35.3 us
    unnamed x16, local copies, waits for them, and re-layouts  16 us
    pallas_call x2, Pallas kernels, with_weights(): pl.pallas_call(kernel, grid=(rows // ROWS,), in_specs=[whole(vec.shape),...  12.3 us
    all_to_all x1, waiting for transfers between devices, exchange(): lax.all_to_all(chunks, 'probe', 0, 0, axis_index_groups=groups, tiled=True)  11.1 us
    pallas_call x1, Pallas kernels, start(): pl.pallas_call(start_kernel, grid=(rows // ROWS,), in_specs=[pl.BlockSpec...  10.3 us
    all_to_all x1, starting transfers between devices, local(): lax.all_to_all(sums, ('head', 'probe'), 0, 0, tiled=True)  9.57 us
    all_to_all x1, waiting for transfers between devices, local(): lax.all_to_all(sums, ('head', 'probe'), 0, 0, tiled=True)  9.27 us
  transfers between devices with their start and end apart: 4, of which 3 were waited for; matrix products, arithmetic and copies ran while one was open for 2% of the time, Pallas kernels for 2%

profile of v1, /device:TPU:1, one launch (start us, length us, event | category | flops | bytes accessed | tf_op | source)
XLA Modules:
  0.0 190.6 jit_solution(5693565693157590833)
XLA Ops:
  0.0 0.0 copy-start
  0.0 1.0 convert_multiply_fusion
  1.0 0.7 convert_element_type.9
  1.8 1.5 collective-permute-start
  3.3 0.0 copy-done
  3.3 1.1 collective-permute-done
  4.5 0.0 copy-start.7
  4.5 3.4 %copy-done.7 = bf16[2,16384,128]{2,1,0:T(8,128)(2,1)S(1)} copy-done((bf16[2,16384,128]{2,1,0:T(8,128)(2,1)S(1)}, bf16[2,16384,128]{2,1,0:T(8,128)(2,1)}, u32[]{:S(2)}) %copy-start.7) | copy-done | bytes 8388632
  7.9 35.3 %attend.1 = (f32[1024,128]{1,0:T(8,128)S(1)}, bf16[1024,256]{1,0:T(8,128)(2,1)S(1)}, bf16[2048,128]{1,0:T(8,128)(2,1)S(1)}, bf16[2048,128]{1,0:T(8,128)(2,1)S(1)}) custom-call(s32[1]{0:T(128)} %bitcast.core, f32[1024,128]{1,0:T(8,128)S(1)} %pad_maximum_fusion.q_ref, f32[8,128]{1,0:T(8,128)S(1)} %pad_maximum_fusion.2.pos_ref, s32[8,2,128]{2,1,0:T(2,128)S(1)} %bitcast.30, ...), custom_call_target="tpu_custom_call" | custom-call | tf_op jit(solution)/shard_map/attend/pallas_call | solution.py:108
  43.2 10.3 %start.1 = (bf16[1024,2048]{1,0:T(8,128)(2,1)S(1)}, bf16[1024,2048]{1,0:T(8,128)(2,1)S(1)}, f32[16,128,128]{2,1,0:T(8,128)S(1)}) custom-call(bf16[1024,256]{1,0:T(8,128)(2,1)S(1)} %get-tuple-element.12.q2_ref, f32[4,2,128]{2,1,0:T(2,128)S(1)} %bitcast.31, s32[1,2048]{1,0:T(1,128)S(1)} %constant_dynamic-slice_fusion.kept_ref, ...), custom_call_target="tpu_custom_call" | custom-call | tf_op jit(solution)/shard_map/start/pallas_call | solution.py:185
  53.5 0.0 copy-start.1
  53.5 1.9 %copy-done.1 = bf16[1024,2048]{1,0:T(8,128)(2,1)} copy-done((bf16[1024,2048]{1,0:T(8,128)(2,1)}, bf16[1024,2048]{1,0:T(8,128)(2,1)S(1)}, u32[]{:S(2)}) %copy-start.1) | copy-done | bytes 4194328
  55.4 0.0 copy-start.4
  55.4 2.0 %copy-done.4 = bf16[1024,2048]{1,0:T(8,128)(2,1)} copy-done((bf16[1024,2048]{1,0:T(8,128)(2,1)}, bf16[1024,2048]{1,0:T(8,128)(2,1)S(1)}, u32[]{:S(2)}) %copy-start.4) | copy-done | bytes 4194328
  57.4 23.8 %all_to_all.25 = f32[16,128,128]{2,1,0:T(8,128)S(1)} all-to-all(f32[16,128,128]{2,1,0:T(8,128)S(1)} %get-tuple-element.16), channel_id=1, replica_groups={{0,2,4,6,8,10,12,14,16,18,20,22,24,26,28,30},{1,3,5,7,9,11,13,15,17,19,..., dimensions={0} | all-to-all | bytes 2097152 | tf_op jit(solution)/shard_map/all_to_all | solution.py:292
  81.2 0.1 reduce_sum.67
  81.2 0.1 broadcast_in_dim.6
  81.3 19.0 %all_to_all.26.vec_ref = f32[16,128,128]{2,1,0:T(8,128)S(1)} all-to-all(f32[16,128,128]{2,1,0:T(8,128)S(1)} %broadcast_in_dim.6), channel_id=1, replica_groups={{0,2,4,6,8,10,12,14,16,18,20,22,24,26,28,30},{1,3,5,7,9,11,13,15,17,19,..., dimensions={0} | all-to-all | bytes 2097152 | tf_op jit(solution)/shard_map/all_to_all | solution.py:292
  100.4 0.0 copy-start.2
  100.4 2.2 %copy-done.2 = bf16[1024,2048]{1,0:T(8,128)(2,1)S(1)} copy-done((bf16[1024,2048]{1,0:T(8,128)(2,1)S(1)}, bf16[1024,2048]{1,0:T(8,128)(2,1)}, u32[]{:S(2)}) %copy-start.2) | copy-done | bytes 4194328
  102.6 0.0 copy-start.5
  102.6 2.2 %copy-done.5 = bf16[1024,2048]{1,0:T(8,128)(2,1)S(1)} copy-done((bf16[1024,2048]{1,0:T(8,128)(2,1)S(1)}, bf16[1024,2048]{1,0:T(8,128)(2,1)}, u32[]{:S(2)}) %copy-start.5) | copy-done | bytes 4194328
  104.8 9.0 %normal.1 = f32[16,128,128]{2,1,0:T(8,128)S(1)} custom-call(f32[16,128,128]{2,1,0:T(8,128)S(1)} %all_to_all.26.vec_ref, bf16[1024,2048]{1,0:T(8,128)(2,1)S(1)} %copy-done.2, bf16[1024,2048]{1,0:T(8,128)(2,1)S(1)} %copy-done.5), custom_call_target="tpu_custom_call" | custom-call | tf_op jit(solution)/shard_map/normal/pallas_call | solution.py:251
  113.8 18.6 %all_to_all.27 = f32[16,128,128]{2,1,0:T(8,128)S(1)} all-to-all(f32[16,128,128]{2,1,0:T(8,128)S(1)} %normal.1), channel_id=1, replica_groups={{0,2,4,6,8,10,12,14,16,18,20,22,24,26,28,30},{1,3,5,7,9,11,13,15,17,19,..., dimensions={0} | all-to-all | bytes 2097152 | tf_op jit(solution)/shard_map/all_to_all | solution.py:292
  132.4 0.1 reduce_sum.69
  132.5 0.7 multiply_reduce_fusion.2
  133.2 1.2 broadcast_in_dim.7
  134.3 3.7 %all-to-all-start.3 = ((f32[16,128,128]{2,1,0:T(8,128)}), f32[16,128,128]{2,1,0:T(8,128)S(1)}, u32[]{:S(2)}, u32[]{:S(2)}) async-start(f32[16,128,128]{2,1,0:T(8,128)} %broadcast_in_dim.7), calls=%async_computation.3 | async-start | bytes 2097152 | tf_op jit(solution)/shard_map/all_to_all | solution.py:292
  138.0 0.1 fusion.4
  138.1 3.0 %collective-permute-start.1 = (f32[2,64,128]{1,2,0:T(8,128)S(1)}, f32[2,64,128]{1,2,0:T(8,128)S(1)}, u32[]{:S(2)}, u32[]{:S(2)}) collective-permute-start(f32[2,64,128]{1,2,0:T(8,128)S(1)} %fusion.4), channel_id=1, source_target_pairs={{0,1},{1,0},{2,3},{3,2},{4,5},{5,4},{6,7},{7,6},{8,9},{9,8},{10,11... | collective-permute-start | bytes 196616 | tf_op jit(solution)/shard_map/ppermute | solution.py:305
  141.2 11.1 %all-to-all-done.3.vec_ref = f32[16,128,128]{2,1,0:T(8,128)S(1)} async-done(((f32[16,128,128]{2,1,0:T(8,128)}), f32[16,128,128]{2,1,0:T(8,128)S(1)}, u32[]{:S(2)}, u32[]{:S(2)}) %all-to-all-start.3) | async-done | bytes 1048608 | tf_op jit(solution)/shard_map/all_to_all | solution.py:292
  152.3 0.0 copy-start.3
  152.3 2.2 %copy-done.3 = bf16[1024,2048]{1,0:T(8,128)(2,1)S(1)} copy-done((bf16[1024,2048]{1,0:T(8,128)(2,1)S(1)}, bf16[1024,2048]{1,0:T(8,128)(2,1)}, u32[]{:S(2)}) %copy-start.3) | copy-done | bytes 4194328
  154.5 0.0 copy-start.6
  154.5 2.2 %copy-done.6 = bf16[1024,2048]{1,0:T(8,128)(2,1)S(1)} copy-done((bf16[1024,2048]{1,0:T(8,128)(2,1)S(1)}, bf16[1024,2048]{1,0:T(8,128)(2,1)}, u32[]{:S(2)}) %copy-start.6) | copy-done | bytes 4194328
  156.7 3.3 %square.1 = f32[1,256]{1,0:T(1,128)S(1)} custom-call(f32[16,128,128]{2,1,0:T(8,128)S(1)} %all-to-all-done.3.vec_ref, bf16[1024,2048]{1,0:T(8,128)(2,1)S(1)} %copy-done.3, bf16[1024,2048]{1,0:T(8,128)(2,1)S(1)} %copy-done.6), custom_call_target="tpu_custom_call" | custom-call | tf_op jit(solution)/shard_map/square/pallas_call | solution.py:251
  159.9 0.6 reduce_sum.72
  160.5 2.7 %select_maximum_fusion = f32[128]{0:T(128)S(1)} fusion(f32[1]{0:T(128)} %bitcast.9, f32[1]{0:T(128)} %bitcast.8, f32[1]{0:T(128)} %bitcast.7, f32[1]{0:T(128)} %bitcast.6), kind=kLoop, calls=%fused_computation.35 | loop fusion | flops 1024 | bytes 528 | tf_op jit(solution)/shard_map/stack | solution.py:310
  163.2 0.7 broadcast_in_dim.8
  163.9 9.6 %all-to-all-start.4 = ((f32[128,1,128]{2,1,0:T(1,128)}), f32[128,1,128]{2,1,0:T(1,128)S(1)}, u32[]{:S(2)}, u32[]{:S(2)}) async-start(f32[128,1,128]{2,1,0:T(1,128)} %broadcast_in_dim.8), calls=%async_computation.4 | async-start | bytes 131072 | tf_op jit(solution)/shard_map/all_to_all | solution.py:312
  173.5 0.0 collective-permute-done.1
  173.5 0.1 broadcast_select_fusion.1
  173.6 9.3 %all-to-all-done.4 = f32[128,1,128]{2,1,0:T(1,128)S(1)} async-done(((f32[128,1,128]{2,1,0:T(1,128)}), f32[128,1,128]{2,1,0:T(1,128)S(1)}, u32[]{:S(2)}, u32[]{:S(2)}) %all-to-all-start.4) | async-done | bytes 65568 | tf_op jit(solution)/shard_map/all_to_all | solution.py:312
  182.9 0.6 fusion.9
  189.9 0.7 copy.11
  (13 shorter events, 0.2 us)
Async XLA Ops:
  0.0 3.3 %copy-start = (s32[2,2048]{1,0:T(2,128)S(1)}, s32[2,2048]{1,0:T(2,128)}, u32[]{:S(2)}) copy-start(s32[2,2048]{1,0:T(2,128)} %param.9) | copy-start | bytes 49156
  1.8 2.7 %collective-permute-start = (f32[516,128]{1,0:T(8,128)S(1)}, f32[516,128]{1,0:T(8,128)S(1)}, u32[]{:S(2)}, u32[]{:S(2)}) collective-permute-start(f32[516,128]{1,0:T(8,128)S(1)} %get-tuple-element.24), channel_id=1, source_target_pairs={{0,1},{1,0},{2,3},{3,2},{4,5},{5,4},{6,7},{7,6},{8,9},{9,8},{10,11... | collective-permute-start | bytes 792584 | tf_op jit(solution)/shard_map/ppermute | solution.py:281
  4.5 3.4 %copy-start.7 = (bf16[2,16384,128]{2,1,0:T(8,128)(2,1)S(1)}, bf16[2,16384,128]{2,1,0:T(8,128)(2,1)}, u32[]{:S(2)}) copy-start(bf16[2,16384,128]{2,1,0:T(8,128)(2,1)} %k_ref.1) | copy-start | bytes 25165828
  53.5 1.9 %copy-start.1 = (bf16[1024,2048]{1,0:T(8,128)(2,1)}, bf16[1024,2048]{1,0:T(8,128)(2,1)S(1)}, u32[]{:S(2)}) copy-start(bf16[1024,2048]{1,0:T(8,128)(2,1)S(1)} %get-tuple-element.17.wh_ref) | copy-start | bytes 12582916
  55.4 2.0 %copy-start.4 = (bf16[1024,2048]{1,0:T(8,128)(2,1)}, bf16[1024,2048]{1,0:T(8,128)(2,1)S(1)}, u32[]{:S(2)}) copy-start(bf16[1024,2048]{1,0:T(8,128)(2,1)S(1)} %get-tuple-element.18.wl_ref) | copy-start | bytes 12582916
  100.4 2.2 %copy-start.2 = (bf16[1024,2048]{1,0:T(8,128)(2,1)S(1)}, bf16[1024,2048]{1,0:T(8,128)(2,1)}, u32[]{:S(2)}) copy-start(bf16[1024,2048]{1,0:T(8,128)(2,1)} %copy-done.1) | copy-start | bytes 12582916
  102.6 2.2 %copy-start.5 = (bf16[1024,2048]{1,0:T(8,128)(2,1)S(1)}, bf16[1024,2048]{1,0:T(8,128)(2,1)}, u32[]{:S(2)}) copy-start(bf16[1024,2048]{1,0:T(8,128)(2,1)} %copy-done.4) | copy-start | bytes 12582916
  134.3 18.0 %all-to-all-start.3 = ((f32[16,128,128]{2,1,0:T(8,128)}), f32[16,128,128]{2,1,0:T(8,128)S(1)}, u32[]{:S(2)}, u32[]{:S(2)}) async-start(f32[16,128,128]{2,1,0:T(8,128)} %broadcast_in_dim.7), calls=%async_computation.3 | async-start | bytes 2097152 | tf_op jit(solution)/shard_map/all_to_all | solution.py:292
  138.1 35.4 %collective-permute-start.1 = (f32[2,64,128]{1,2,0:T(8,128)S(1)}, f32[2,64,128]{1,2,0:T(8,128)S(1)}, u32[]{:S(2)}, u32[]{:S(2)}) collective-permute-start(f32[2,64,128]{1,2,0:T(8,128)S(1)} %fusion.4), channel_id=1, source_target_pairs={{0,1},{1,0},{2,3},{3,2},{4,5},{5,4},{6,7},{7,6},{8,9},{9,8},{10,11... | collective-permute-start | bytes 196616 | tf_op jit(solution)/shard_map/ppermute | solution.py:305
  152.3 2.2 %copy-start.3 = (bf16[1024,2048]{1,0:T(8,128)(2,1)S(1)}, bf16[1024,2048]{1,0:T(8,128)(2,1)}, u32[]{:S(2)}) copy-start(bf16[1024,2048]{1,0:T(8,128)(2,1)} %copy-done.1) | copy-start | bytes 12582916
  154.5 2.2 %copy-start.6 = (bf16[1024,2048]{1,0:T(8,128)(2,1)S(1)}, bf16[1024,2048]{1,0:T(8,128)(2,1)}, u32[]{:S(2)}) copy-start(bf16[1024,2048]{1,0:T(8,128)(2,1)} %copy-done.4) | copy-start | bytes 12582916
  163.9 19.0 %all-to-all-start.4 = ((f32[128,1,128]{2,1,0:T(1,128)}), f32[128,1,128]{2,1,0:T(1,128)S(1)}, u32[]{:S(2)}, u32[]{:S(2)}) async-start(f32[128,1,128]{2,1,0:T(1,128)} %broadcast_in_dim.8), calls=%async_computation.4 | async-start | bytes 131072 | tf_op jit(solution)/shard_map/all_to_all | solution.py:312

commit v2 on v0

v2 whole, which is shorter than its diff:
```python
import math

import jax
import jax.numpy as jnp
from jax import lax
from jax.experimental import pallas as pl
from jax.experimental.pallas import tpu as pltpu
from jax.sharding import PartitionSpec as P

HD = 128
LANES = 128
BLOCK = 2048
ROWS = 256
PICK = 256
LIMIT = 2.0**40
MIB = 1024 * 1024
f32 = jnp.float32
bf16 = jnp.bfloat16
NT = (((1,), (1,)), ((), ()))
NN = (((1,), (0,)), ((), ()))


def dot(left, right, dims=NN):
    return lax.dot_general(left, right, dims, preferred_element_type=f32)


def halves(wide):
    high = wide.astype(bf16)
    return high, (wide - high.astype(f32)).astype(bf16)


def stacked(wide):
    return jnp.concatenate(halves(wide), axis=0)


def whole(shape):
    return pl.BlockSpec(shape, lambda *ids: (0,) * len(shape))


def params():
    return pltpu.CompilerParams(vmem_limit_bytes=56 * MIB)


def columns_of(rows):
    return jnp.transpose(rows).astype(jnp.int32)


def stack_columns(cols, first, count):
    return jnp.concatenate([cols[:, i : i + 1] for i in range(first, first + count)], axis=0)


def attend_kernel(core, mine_ref, other_ref, kept_ref, k_ref, v_ref, k_any, v_any, t_ref, q2_ref, pos_ref, kk_ref, kv_ref, m_ref, acc_ref, k2_ref, v2_ref, sem):
    step = pl.program_id(0)
    steps = pl.num_programs(0)
    rows = q2_ref.shape[0]
    own = rows // 2
    tiles = rows // ROWS
    slots = PICK // 8

    @pl.when(step == 0)
    def _():
        for part, ref in enumerate((mine_ref.at[0], other_ref)):
            high, low = halves(ref[:own, :])
            q2_ref[pl.ds(part * own, own), :HD] = high
            q2_ref[pl.ds(part * own, own), HD:] = low
            pos_ref[pl.ds(part * own // LANES, own // LANES), :] = ref[own:, :]
        acc_ref[...] = jnp.zeros(acc_ref.shape, f32)
        v2_ref[:, HD:] = jnp.ones((BLOCK, HD), bf16)

    def load(keys, values):
        k2_ref[:, :HD] = keys
        k2_ref[:, HD:] = keys
        v2_ref[:, :HD] = values

    load(k_ref[0], v_ref[0])

    per = BLOCK // 8
    kept_row = kept_ref[pl.ds(core[0], 1), pl.ds(pl.multiple_of(step * per, per), per)] - step * BLOCK
    lane = lax.broadcasted_iota(jnp.int32, (slots, PICK), 1)
    for half in range(per // LANES):
        col = jnp.transpose(jnp.broadcast_to(kept_row[:, half * LANES : (half + 1) * LANES], (LANES, LANES)))[:, :1]
        for piece in range(LANES // slots):
            at = (half * LANES + piece * slots) * 8
            hot = jnp.where(lane == col[piece * slots : (piece + 1) * slots, :] - at, 1.0, 0.0).astype(bf16)
            both = jnp.concatenate([k_ref[0, at : at + PICK, :], v_ref[0, at : at + PICK, :]], axis=1)
            got = dot(hot, both).astype(bf16)
            here = pl.ds(half * LANES + piece * slots, slots)
            kk_ref[here, :] = got[:, :HD]
            kv_ref[here, :] = got[:, HD:]

    def scores_of(tile, base, masked):
        scores = dot(q2_ref[pl.ds(tile * ROWS, ROWS), :], k2_ref[...], NT)
        if masked:
            cols = columns_of(pos_ref[...]) - base
            pos = stack_columns(cols, tile * ROWS // LANES, ROWS // LANES)
            lane = lax.broadcasted_iota(jnp.int32, scores.shape, 1)
            scores = jnp.where(lane <= pos, scores, -jnp.inf)
        return scores

    def go(first, masked):
        for tile in range(tiles):
            here = pl.ds(tile * ROWS, ROWS)
            scores = scores_of(tile, step * BLOCK, masked)
            if first:
                m_ref[here, :] = jnp.broadcast_to(jnp.max(scores, axis=1, keepdims=True), (ROWS, LANES))
            expo = jnp.exp2(scores - m_ref[here, :1]).astype(bf16)
            acc_ref[here, :] += dot(expo, v2_ref[...])

    half = steps // 2

    @pl.when(step == 0)
    def _():
        go(True, False)

    @pl.when((step > 0) & (step < half))
    def _():
        go(False, False)

    @pl.when(step >= half)
    def _():
        go(False, True)

    @pl.when((step == steps - 1) & jnp.logical_not(jnp.max(acc_ref[:, HD:]) <= LIMIT))
    def _():
        m_ref[...] = jnp.full(m_ref.shape, -jnp.inf, f32)
        acc_ref[...] = jnp.zeros(acc_ref.shape, f32)

        def block(j, carry):
            here = pl.ds(pl.multiple_of(j * BLOCK, BLOCK), BLOCK)
            for any_ref, to in ((k_any, k2_ref.at[:, :HD]), (k_any, k2_ref.at[:, HD:]), (v_any, v2_ref.at[:, :HD])):
                copy = pltpu.make_async_copy(any_ref.at[core[0], here, :], to, sem)
                copy.start()
                copy.wait()
            for tile in range(tiles):
                rows_here = pl.ds(tile * ROWS, ROWS)
                scores = scores_of(tile, j * BLOCK, True)
                old = m_ref[rows_here, :]
                new = jnp.maximum(old, jnp.max(scores, axis=1, keepdims=True))
                m_ref[rows_here, :] = new
                expo = jnp.exp2(scores - new[:, :1]).astype(bf16)
                fade = jnp.exp2(old - new)
                both = jnp.concatenate([fade, fade], axis=1)
                acc_ref[rows_here, :] = acc_ref[rows_here, :] * both + dot(expo, v2_ref[...])
            return carry

        lax.fori_loop(0, steps, block, 0)

    @pl.when(step == steps - 1)
    def _():
        t_ref[...] = acc_ref[:, :HD] / acc_ref[:, HD:]


def attend(core, packed, other, kept, keys, values):
    own = packed.shape[1] - packed.shape[1] % LANES
    rows = 2 * own
    steps = keys.shape[1] // BLOCK
    count = kept.shape[1]
    per = BLOCK // 8
    return pl.pallas_call(
        attend_kernel,
        grid_spec=pltpu.PrefetchScalarGridSpec(
            num_scalar_prefetch=1,
            grid=(steps,),
            in_specs=[
                pl.BlockSpec((1,) + packed.shape[1:], lambda j, c: (c[0], 0, 0)),
                whole(other.shape),
                whole(kept.shape),
                pl.BlockSpec((1, BLOCK, HD), lambda j, c: (c[0], j, 0)),
                pl.BlockSpec((1, BLOCK, HD), lambda j, c: (c[0], j, 0)),
                pl.BlockSpec(memory_space=pl.ANY),
                pl.BlockSpec(memory_space=pl.ANY),
            ],
            out_specs=[
                whole((rows, HD)),
                whole((rows, 2 * HD)),
                whole((rows // LANES, LANES)),
                pl.BlockSpec((per, HD), lambda j, c: (j, 0)),
                pl.BlockSpec((per, HD), lambda j, c: (j, 0)),
            ],
            scratch_shapes=[
                pltpu.VMEM((rows, LANES), f32),
                pltpu.VMEM((rows, 2 * HD), f32),
                pltpu.VMEM((BLOCK, 2 * HD), bf16),
                pltpu.VMEM((BLOCK, 2 * HD), bf16),
                pltpu.SemaphoreType.DMA,
            ],
        ),
        out_shape=[
            jax.ShapeDtypeStruct((rows, HD), f32),
            jax.ShapeDtypeStruct((rows, 2 * HD), bf16),
            jax.ShapeDtypeStruct((rows // LANES, LANES), f32),
            jax.ShapeDtypeStruct((count, HD), bf16),
            jax.ShapeDtypeStruct((count, HD), bf16),
        ],
        compiler_params=params(),
        name="attend",
    )(core, packed, other, kept, keys, values, keys, values)


def add_chunks(z_ref, part, first):
    for chunk in range(z_ref.shape[0]):
        cut = part[:, chunk * LANES : (chunk + 1) * LANES]
        z_ref[chunk] = cut if first else z_ref[chunk] + cut


def first_and_rest(tile, body):
    @pl.when(tile == 0)
    def _():
        body(True)

    @pl.when(tile > 0)
    def _():
        body(False)


def start_kernel(core, q2_ref, pos_ref, kept_ref, kk_ref, kv_ref, t_ref, e_ref, over_ref, z_ref, k2_ref):
    tile = pl.program_id(0)

    @pl.when(tile == 0)
    def _():
        k2_ref[:, :HD] = kk_ref[...]
        k2_ref[:, HD:] = kk_ref[...]

    scores = dot(q2_ref[...], k2_ref[...], NT)
    pos = stack_columns(columns_of(pos_ref[...]), 0, ROWS // LANES)
    scores = jnp.where(kept_ref[pl.ds(core[0], 1), :] <= pos, scores, -jnp.inf)
    expo = jnp.exp2(scores - jnp.max(scores, axis=1, keepdims=True))
    over = 1.0 / jnp.sum(expo, axis=1, keepdims=True)
    high, low = halves(expo)
    e_ref[...] = high
    gap = t_ref[...] - (dot(high, kv_ref[...]) + dot(low, kv_ref[...])) * over
    over_ref[...] = jnp.transpose(jnp.broadcast_to(over, (ROWS, LANES)))[:8, :]
    gap_t = stacked(jnp.transpose(gap * over))

    def body(first):
        two = dot(gap_t, high)
        add_chunks(z_ref, two[:HD] + two[HD:] + dot(gap_t[:HD], low), first)

    first_and_rest(tile, body)


def start(core, q2, pos, kept, kept_keys, kept_values, target):
    rows = q2.shape[0]
    count = kept_keys.shape[0]
    return pl.pallas_call(
        start_kernel,
        grid_spec=pltpu.PrefetchScalarGridSpec(
            num_scalar_prefetch=1,
            grid=(rows // ROWS,),
            in_specs=[
                pl.BlockSpec((ROWS, 2 * HD), lambda i, c: (i, 0)),
                pl.BlockSpec((None, ROWS // LANES, LANES), lambda i, c: (i, 0, 0)),
                whole(kept.shape),
                whole((count, HD)),
                whole((count, HD)),
                pl.BlockSpec((ROWS, HD), lambda i, c: (i, 0)),
            ],
            out_specs=[
                pl.BlockSpec((ROWS, count), lambda i, c: (i, 0)),
                pl.BlockSpec((8, ROWS), lambda i, c: (0, i)),
                whole((count // LANES, HD, LANES)),
            ],
            scratch_shapes=[pltpu.VMEM((count, 2 * HD), bf16)],
        ),
        out_shape=[
            jax.ShapeDtypeStruct((rows, count), bf16),
            jax.ShapeDtypeStruct((8, rows), f32),
            jax.ShapeDtypeStruct((count // LANES, HD, LANES), f32),
        ],
        compiler_params=params(),
        name="start",
    )(core, q2, pos.reshape(rows // ROWS, ROWS // LANES, LANES), kept, kept_keys, kept_values, target)


def load_vector(vec_ref, two_ref):
    for chunk in range(vec_ref.shape[0]):
        two_ref[:, chunk * LANES : (chunk + 1) * LANES] = stacked(vec_ref[chunk])


def normal_kernel(vec_ref, e_ref, over_ref, z_ref, two_ref):
    tile = pl.program_id(0)

    @pl.when(tile == 0)
    def _():
        load_vector(vec_ref, two_ref)

    expo = e_ref[...]
    over = over_ref[:1, :]
    two = dot(two_ref[...], expo, NT)
    image = stacked((two[:HD] + two[HD:]) * (over * over))

    def body(first):
        back = dot(image, expo)
        add_chunks(z_ref, back[:HD] + back[HD:], first)

    first_and_rest(tile, body)


def square_kernel(vec_ref, e_ref, over_ref, sums_ref, s_ref, two_ref, total_ref):
    tile = pl.program_id(0)

    @pl.when(tile == 0)
    def _():
        load_vector(vec_ref, two_ref)
        total_ref[...] = jnp.zeros(total_ref.shape, f32)

    two = dot(two_ref[...], e_ref[...], NT)
    image = (two[:HD] + two[HD:]) * over_ref[:1, :]
    total_ref[...] += jnp.sum(image * image, axis=0, keepdims=True)

    @pl.when(tile == pl.num_programs(0) - 1)
    def _():
        last = total_ref[...]
        last = sum(last[:, i * LANES : (i + 1) * LANES] for i in range(ROWS // LANES))
        row = lax.broadcasted_iota(jnp.int32, sums_ref.shape, 0)
        lane = lax.broadcasted_iota(jnp.int32, sums_ref.shape, 1)
        sums = jnp.sum(jnp.where(row == 3, last, sums_ref[...]), axis=1, keepdims=True)
        line = jnp.sum(jnp.where(row == lane, sums, 0.0), axis=0, keepdims=True)
        s_ref[...] = jnp.broadcast_to(line[None], s_ref.shape)


def with_weights(kernel, name, out, vec, expo, over, *more, scratch=()):
    rows, count = expo.shape
    return pl.pallas_call(
        kernel,
        grid=(rows // ROWS,),
        in_specs=[
            whole(vec.shape),
            pl.BlockSpec((ROWS, count), lambda i: (i, 0)),
            pl.BlockSpec((8, ROWS), lambda i: (0, i)),
        ]
        + [whole(a.shape) for a in more],
        out_specs=whole(out),
        out_shape=jax.ShapeDtypeStruct(out, f32),
        scratch_shapes=[pltpu.VMEM((2 * HD, count), bf16), *scratch],
        compiler_params=params(),
        name=name,
    )(vec, expo, over, *more)


def fold_kernel(parts_ref, chunk_ref, copies_ref):
    total = jnp.sum(parts_ref[...], axis=0)
    chunk_ref[...] = total
    copies_ref[...] = jnp.broadcast_to(total[None], copies_ref.shape)


def fold(parts):
    return pl.pallas_call(
        fold_kernel,
        in_specs=[whole(parts.shape)],
        out_specs=[whole(parts.shape[1:]), whole(parts.shape)],
        out_shape=[jax.ShapeDtypeStruct(parts.shape[1:], f32), jax.ShapeDtypeStruct(parts.shape, f32)],
        compiler_params=params(),
        name="fold",
    )(parts)


def fold_image_kernel(ridge, core, parts_ref, res_ref, copies_ref, sums_ref, keep_ref, send_ref, turn_ref):
    res = res_ref[...]
    total = jnp.sum(parts_ref[...], axis=0) + ridge * res
    copies_ref[...] = jnp.broadcast_to(total[None], copies_ref.shape)
    sums_ref[...] = jnp.zeros(sums_ref.shape, f32)
    sums_ref[0:1, :] = jnp.sum(res * res, axis=0, keepdims=True)
    sums_ref[1:2, :] = jnp.sum(res * total, axis=0, keepdims=True)
    sums_ref[2:3, :] = jnp.sum(total * total, axis=0, keepdims=True)
    half = keep_ref.shape[1]
    for i, chunk in enumerate((res, total)):
        turn_ref[...] = jnp.transpose(chunk)
        keep_ref[i] = turn_ref[pl.ds(pl.multiple_of(core[0] * half, half), half), :]
        send_ref[i] = turn_ref[pl.ds(pl.multiple_of((1 - core[0]) * half, half), half), :]


def fold_image(core, ridge, parts, res):
    half = (2, parts.shape[2] // 2, HD)
    return pl.pallas_call(
        lambda *refs: fold_image_kernel(ridge, *refs),
        grid_spec=pltpu.PrefetchScalarGridSpec(
            num_scalar_prefetch=1,
            grid=(1,),
            in_specs=[whole(parts.shape), whole(res.shape)],
            out_specs=[whole(parts.shape), whole((8, LANES)), whole(half), whole(half)],
            scratch_shapes=[pltpu.VMEM(res.shape, f32)],
        ),
        out_shape=[
            jax.ShapeDtypeStruct(parts.shape, f32),
            jax.ShapeDtypeStruct((8, LANES), f32),
            jax.ShapeDtypeStruct(half, f32),
            jax.ShapeDtypeStruct(half, f32),
        ],
        compiler_params=params(),
        name="fold_image",
    )(core, parts, res)


def finish_kernel(ridge, core, sums_ref, keep_ref, got_ref, out_ref):
    sums = jnp.sum(sums_ref[...], axis=0)
    lane = lax.broadcasted_iota(jnp.int32, sums.shape, 1)
    rr, rn, nn, ww = (jnp.sum(jnp.where(lane == i, sums, 0.0), axis=1, keepdims=True) for i in range(4))
    alpha = rr / rn
    new = rr - 2.0 * alpha * rn + alpha * alpha * nn
    beta = new / rr
    grow = 1.0 + beta
    curve = grow * grow * rn - 2.0 * alpha * grow * nn + alpha * alpha * (ww + ridge * nn)
    step = new / curve
    left = alpha + step * grow
    right = -step * alpha
    out_ref[core[0]] = left * keep_ref[0] + right * keep_ref[1]
    out_ref[1 - core[0]] = left * got_ref[0] + right * got_ref[1]


def finish(core, ridge, sums, keep, got):
    return pl.pallas_call(
        lambda *refs: finish_kernel(ridge, *refs),
        grid_spec=pltpu.PrefetchScalarGridSpec(
            num_scalar_prefetch=1,
            grid=(1,),
            in_specs=[whole(sums.shape), whole(keep.shape), whole(got.shape)],
            out_specs=whole(keep.shape),
        ),
        out_shape=jax.ShapeDtypeStruct(keep.shape, f32),
        compiler_params=params(),
        name="finish",
    )(core, sums, keep, got)


def local(history_keys, history_values, queries, positions, kept_index):
    count = kept_index.shape[1]
    own_rows = queries.shape[1]
    devices = lax.axis_size("probe")
    chips = devices // 2
    everyone = lax.axis_size("head") * devices
    ridge = own_rows * devices / (count * count)
    index = lax.rem(lax.axis_index("probe"), 2)
    core = index.astype(jnp.int32).reshape(1)
    swap = [(i, i ^ 1) for i in range(devices)]
    groups = [[2 * i + c for i in range(chips)] for c in range(2)]

    scaled = queries.astype(f32) * (math.log2(math.e) / math.sqrt(HD))
    packed = jnp.concatenate([scaled, positions.astype(f32).reshape(2, own_rows // LANES, LANES)], axis=1)
    other = lax.ppermute(lax.dynamic_index_in_dim(packed, 1 - index, 0, keepdims=False), "probe", swap)
    target, q2, pos, kept_keys, kept_values = attend(core, packed, other, kept_index, history_keys, history_values)
    expo, over, z = start(core, q2, pos, kept_index, kept_keys, kept_values, target)

    def exchange(chunks):
        return lax.all_to_all(chunks, "probe", 0, 0, axis_index_groups=groups, tiled=True)

    res, copies = fold(exchange(z))
    z = with_weights(normal_kernel, "normal", z.shape, exchange(copies), expo, over)
    copies, sums, keep, send = fold_image(core, ridge, exchange(z), res)
    got = lax.ppermute(send, "probe", swap)
    sums = with_weights(
        square_kernel, "square", (everyone, 1, LANES), exchange(copies), expo, over, sums, scratch=[pltpu.VMEM((1, ROWS), f32)]
    )
    sums = lax.all_to_all(sums, ("head", "probe"), 0, 0, tiled=True)
    return finish(core, ridge, sums, keep, got)


def solution(mesh):
    return jax.shard_map(
        local,
        mesh=mesh,
        in_specs=(
            P("head", None, None),
            P("head", None, None),
            P("head", "probe", None),
            P("head", "probe"),
            P("head", None),
        ),
        out_specs=P("head", "probe", None),
        check_vma=False,
    )
```

time: 706 us -> 227 us (0.32); the launches traced: 694 us -> 224 us
  waiting for transfers between devices: 328 us -> 19 us
  local copies, waits for them, and re-layouts: 139 us -> 2.32 us
  matrix products: 135 us -> 0 us
  blocking collectives: 24.9 us -> 117 us
  Pallas kernels: 0 us -> 61.4 us
  other arithmetic: 49.2 us -> 2.54 us
  starting transfers between devices: 0.09 us -> 21.1 us
  between operations: 17.5 us -> 0.07 us
    psum x3 -> x0, waiting for transfers between devices: 328 us -> none  [total_terms(): return lax.psum(term, 'probe')]
    gather x2 -> x0, local copies, waits for them, and re-layouts: 139 us -> none  [the longest x1 69.7 us: local(): jnp.take_along_axis(history_keys, kept_index[:, :, None], axis=1)]
    dot_general x11 -> x0, matrix products: 135 us -> none  [the longest x3 40.1 us: forward(): jnp.einsum('hpk,hkd->hpd', weights, vec, precision=HIGH, preferred_elemen...]
    all_to_all x0 -> x3, blocking collectives: none -> 117 us  [exchange(): lax.all_to_all(chunks, 'probe', 0, 0, axis_index_groups=groups, tiled=True)]
    pallas_call x0 -> x7, Pallas kernels: none -> 61.4 us  [the longest x1 30.5 us: attend(): pl.pallas_call(attend_kernel, grid_spec=pltpu.PrefetchScalarGridSpec(num_...]
    reduce_sum x5 -> x0, other arithmetic: 40 us -> none  [the longest x2 31.1 us: masked_parts(): return (expo, jnp.sum(expo, axis=-1, keepdims=True))]
    psum x3 -> x0, blocking collectives: 24.9 us -> none  [global_dot(): return lax.psum(jnp.sum(left * right), 'head')]
    all_to_all x0 -> x2, waiting for transfers between devices: none -> 18.7 us  [the longest x1 9.4 us: local(): sums = lax.all_to_all(sums, ('head', 'probe'), 0, 0, tiled=True)]
  transfers between devices with their start and end apart: 3 -> 4, of which waited for: 3 -> 3; matrix products, arithmetic and copies ran while one was open for 0% -> 0% of each run, Pallas kernels for 0% -> 2%
where the time goes in v2:
time: 227 us; the launch traced here: 224 us
  blocking collectives  117 us (52%)
  Pallas kernels  61.4 us (27%)
  starting transfers between devices  21.1 us (9%)
  waiting for transfers between devices  19 us (8%)
  other arithmetic  2.54 us (1%)
  local copies, waits for them, and re-layouts  2.32 us (1%)
    all_to_all x3, blocking collectives, exchange(): lax.all_to_all(chunks, 'probe', 0, 0, axis_index_groups=groups, tiled=True)  117 us
    pallas_call x1, Pallas kernels, attend(): pl.pallas_call(attend_kernel, grid_spec=pltpu.PrefetchScalarGridSpec(num_...  30.5 us
    pallas_call x2, Pallas kernels, with_weights(): pl.pallas_call(kernel, grid=(rows // ROWS,), in_specs=[whole(vec.shape),...  12.3 us
    pallas_call x1, Pallas kernels, start(): pl.pallas_call(start_kernel, grid_spec=pltpu.PrefetchScalarGridSpec(num_s...  12 us
    all_to_all x1, starting transfers between devices, local(): sums = lax.all_to_all(sums, ('head', 'probe'), 0, 0, tiled=True)  11.8 us
    all_to_all x1, waiting for transfers between devices, local(): sums = lax.all_to_all(sums, ('head', 'probe'), 0, 0, tiled=True)  9.4 us
    all_to_all x1, waiting for transfers between devices, exchange(): lax.all_to_all(chunks, 'probe', 0, 0, axis_index_groups=groups, tiled=True)  9.3 us
  transfers between devices with their start and end apart: 4, of which 3 were waited for; matrix products, arithmetic and copies ran while one was open for 0% of the time, Pallas kernels for 2%

profile of v2, /device:TPU:1, one launch (start us, length us, event | category | flops | bytes accessed | tf_op | source)
XLA Modules:
  0.0 224.0 jit_solution(6030544539830603642)
XLA Ops:
  0.0 0.7 convert_element_type.7
  0.7 1.0 convert_multiply_fusion
  1.7 1.5 collective-permute-start
  3.2 0.8 pad_maximum_fusion.mine_ref
  4.1 0.3 collective-permute-done.other_ref
  4.4 0.0 copy-start.1
  4.4 0.7 copy-done.1
  5.1 30.5 %attend.1 = (f32[1024,128]{1,0:T(8,128)}, bf16[1024,256]{1,0:T(8,128)(2,1)}, f32[8,128]{1,0:T(8,128)}, bf16[2048,128]{1,0:T(8,128)(2,1)}, bf16[2048,128]{1,0:T(8,128)(2,1)}) custom-call(s32[1]{0:T(128)} %bitcast.core.refs_0_, f32[2,516,128]{2,1,0:T(8,128)} %pad_maximum_fusion.mine_ref, f32[516,128]{1,0:T(8,128)} %copy-done.1, s32[2,2048]{1,0:T(2,128)} %kept_ref.3, ...), custom_call_target="tpu_custom_call" | custom-call | tf_op jit(solution)/shard_map/attend/pallas_call | solution.py:159
  35.7 12.0 %start.1 = (bf16[1024,2048]{1,0:T(8,128)(2,1)}, f32[8,1024]{1,0:T(8,128)}, f32[16,128,128]{2,1,0:T(8,128)}) custom-call(s32[1]{0:T(128)} %bitcast.core.refs_0_, bf16[1024,256]{1,0:T(8,128)(2,1)} %get-tuple-element.19.q2_ref, f32[4,2,128]{2,1,0:T(2,128)} %bitcast.4, s32[2,2048]{1,0:T(2,128)} %kept_ref.3, bf16[2048,128]{1,0:T(8,128)(2,1)} %get-tuple-element.21.kk_ref, ...), custom_call_target="tpu_custom_call" | custom-call | tf_op jit(solution)/shard_map/start/pallas_call | solution.py:245
  47.7 79.4 %all_to_all.25.parts_ref = f32[16,128,128]{2,1,0:T(8,128)} all-to-all(f32[16,128,128]{2,1,0:T(8,128)} %get-tuple-element.24), channel_id=1, replica_groups={{0,2,4,6,8,10,12,14,16,18,20,22,24,26,28,30},{1,3,5,7,9,11,13,15,17,19,..., dimensions={0} | all-to-all | bytes 2097152 | tf_op jit(solution)/shard_map/all_to_all | solution.py:445
  127.1 2.3 %fold.1 = (f32[128,128]{1,0:T(8,128)}, f32[16,128,128]{2,1,0:T(8,128)}) custom-call(f32[16,128,128]{2,1,0:T(8,128)} %all_to_all.25.parts_ref), custom_call_target="tpu_custom_call" | custom-call | tf_op jit(solution)/shard_map/fold/pallas_call | solution.py:348
  129.4 19.7 %all_to_all.26.vec_ref = f32[16,128,128]{2,1,0:T(8,128)} all-to-all(f32[16,128,128]{2,1,0:T(8,128)} %get-tuple-element.25), channel_id=1, replica_groups={{0,2,4,6,8,10,12,14,16,18,20,22,24,26,28,30},{1,3,5,7,9,11,13,15,17,19,..., dimensions={0} | all-to-all | bytes 2097152 | tf_op jit(solution)/shard_map/all_to_all | solution.py:445
  149.1 6.9 %normal.1 = f32[16,128,128]{2,1,0:T(8,128)} custom-call(f32[16,128,128]{2,1,0:T(8,128)} %all_to_all.26.vec_ref, bf16[1024,2048]{1,0:T(8,128)(2,1)} %get-tuple-element.26.e_ref, f32[8,1024]{1,0:T(8,128)} %get-tuple-element.27.over_ref), custom_call_target="tpu_custom_call" | custom-call | tf_op jit(solution)/shard_map/normal/pallas_call | solution.py:324
  156.0 18.4 %all_to_all.27.refs_1_ = f32[16,128,128]{2,1,0:T(8,128)} all-to-all(f32[16,128,128]{2,1,0:T(8,128)} %normal.1), channel_id=1, replica_groups={{0,2,4,6,8,10,12,14,16,18,20,22,24,26,28,30},{1,3,5,7,9,11,13,15,17,19,..., dimensions={0} | all-to-all | bytes 2097152 | tf_op jit(solution)/shard_map/all_to_all | solution.py:445
  174.4 2.4 %fold_image.1 = (f32[16,128,128]{2,1,0:T(8,128)}, f32[8,128]{1,0:T(8,128)}, f32[2,64,128]{2,1,0:T(8,128)}, f32[2,64,128]{2,1,0:T(8,128)}) custom-call(s32[1]{0:T(128)} %bitcast.core.refs_0_, f32[16,128,128]{2,1,0:T(8,128)} %all_to_all.27.refs_1_, f32[128,128]{1,0:T(8,128)} %get-tuple-element.28.refs_2_), custom_call_target="tpu_custom_call" | custom-call | tf_op jit(solution)/shard_map/fold_image/pallas_call | solution.py:375
  176.9 3.7 %all-to-all-start.3 = ((f32[16,128,128]{2,1,0:T(8,128)}), f32[16,128,128]{2,1,0:T(8,128)S(1)}, u32[]{:S(2)}, u32[]{:S(2)}) async-start(f32[16,128,128]{2,1,0:T(8,128)} %get-tuple-element.29), calls=%async_computation.3 | async-start | bytes 2097152 | tf_op jit(solution)/shard_map/all_to_all | solution.py:445
  180.5 4.2 %collective-permute-start.1 = (f32[2,64,128]{2,1,0:T(8,128)}, f32[2,64,128]{2,1,0:T(8,128)S(1)}, u32[]{:S(2)}, u32[]{:S(2)}) collective-permute-start(f32[2,64,128]{2,1,0:T(8,128)} %get-tuple-element.32), channel_id=1, source_target_pairs={{0,1},{1,0},{2,3},{3,2},{4,5},{5,4},{6,7},{7,6},{8,9},{9,8},{10,11... | collective-permute-start | bytes 196616 | tf_op jit(solution)/shard_map/ppermute | solution.py:450
  184.7 9.3 %all-to-all-done.3.vec_ref = f32[16,128,128]{2,1,0:T(8,128)S(1)} async-done(((f32[16,128,128]{2,1,0:T(8,128)}), f32[16,128,128]{2,1,0:T(8,128)S(1)}, u32[]{:S(2)}, u32[]{:S(2)}) %all-to-all-start.3) | async-done | bytes 1048608 | tf_op jit(solution)/shard_map/all_to_all | solution.py:445
  194.0 0.0 copy-start
  194.0 1.0 copy-done
  194.9 5.4 %square.1 = f32[128,1,128]{2,1,0:T(1,128)} custom-call(f32[16,128,128]{2,1,0:T(8,128)} %copy-done, bf16[1024,2048]{1,0:T(8,128)(2,1)} %get-tuple-element.26.e_ref, f32[8,1024]{1,0:T(8,128)} %get-tuple-element.27.over_ref, f32[8,128]{1,0:T(8,128)} %get-tuple-element.30.sums_ref), custom_call_target="tpu_custom_call" | custom-call | tf_op jit(solution)/shard_map/square/pallas_call | solution.py:324
  200.3 11.8 %all-to-all-start.4 = ((f32[128,1,128]{2,1,0:T(1,128)}), f32[128,1,128]{2,1,0:T(1,128)S(1)}, u32[]{:S(2)}, u32[]{:S(2)}) async-start(f32[128,1,128]{2,1,0:T(1,128)} %square.1), calls=%async_computation.4 | async-start | bytes 131072 | tf_op jit(solution)/shard_map/all_to_all | solution.py:454
  212.1 0.0 collective-permute-done.1.refs_3_
  212.1 0.0 copy-start.3
  212.2 9.4 %all-to-all-done.4.refs_1_ = f32[128,1,128]{2,1,0:T(1,128)S(1)} async-done(((f32[128,1,128]{2,1,0:T(1,128)}), f32[128,1,128]{2,1,0:T(1,128)S(1)}, u32[]{:S(2)}, u32[]{:S(2)}) %all-to-all-start.4) | async-done | bytes 65568 | tf_op jit(solution)/shard_map/all_to_all | solution.py:454
  221.6 0.0 copy-start.2
  221.6 0.0 copy-done.3
  221.6 0.6 copy-done.2
  222.2 1.8 finish.1
  (2 shorter events, 0.0 us)
Async XLA Ops:
  1.7 2.7 %collective-permute-start = (f32[516,128]{1,0:T(8,128)S(1)}, f32[516,128]{1,0:T(8,128)S(1)}, u32[]{:S(2)}, u32[]{:S(2)}) collective-permute-start(f32[516,128]{1,0:T(8,128)S(1)} %fusion.1), channel_id=1, source_target_pairs={{0,1},{1,0},{2,3},{3,2},{4,5},{5,4},{6,7},{7,6},{8,9},{9,8},{10,11... | collective-permute-start | bytes 792584 | tf_op jit(solution)/shard_map/ppermute | solution.py:440
  4.4 0.7 copy-start.1
  176.9 17.1 %all-to-all-start.3 = ((f32[16,128,128]{2,1,0:T(8,128)}), f32[16,128,128]{2,1,0:T(8,128)S(1)}, u32[]{:S(2)}, u32[]{:S(2)}) async-start(f32[16,128,128]{2,1,0:T(8,128)} %get-tuple-element.29), calls=%async_computation.3 | async-start | bytes 2097152 | tf_op jit(solution)/shard_map/all_to_all | solution.py:445
  180.5 31.6 %collective-permute-start.1 = (f32[2,64,128]{2,1,0:T(8,128)}, f32[2,64,128]{2,1,0:T(8,128)S(1)}, u32[]{:S(2)}, u32[]{:S(2)}) collective-permute-start(f32[2,64,128]{2,1,0:T(8,128)} %get-tuple-element.32), channel_id=1, source_target_pairs={{0,1},{1,0},{2,3},{3,2},{4,5},{5,4},{6,7},{7,6},{8,9},{9,8},{10,11... | collective-permute-start | bytes 196616 | tf_op jit(solution)/shard_map/ppermute | solution.py:450
  194.0 1.0 copy-start
  200.3 21.2 %all-to-all-start.4 = ((f32[128,1,128]{2,1,0:T(1,128)}), f32[128,1,128]{2,1,0:T(1,128)S(1)}, u32[]{:S(2)}, u32[]{:S(2)}) async-start(f32[128,1,128]{2,1,0:T(1,128)} %square.1), calls=%async_computation.4 | async-start | bytes 131072 | tf_op jit(solution)/shard_map/all_to_all | solution.py:454
  212.1 9.4 %copy-start.3 = (f32[2,64,128]{2,1,0:T(8,128)}, f32[2,64,128]{2,1,0:T(8,128)S(1)}, u32[]{:S(2)}) copy-start(f32[2,64,128]{2,1,0:T(8,128)S(1)} %collective-permute-done.1.refs_3_) | copy-start | bytes 196612
  221.6 0.6 copy-start.2

commit v3 on v2

v3 whole, which is shorter than its diff:
```python
import math

import jax
import jax.numpy as jnp
from jax import lax
from jax.experimental import pallas as pl
from jax.experimental.pallas import tpu as pltpu
from jax.sharding import Mesh
from jax.sharding import PartitionSpec as P

HD = 128
LANES = 128
BLOCK = 2048
ROWS = 256
PICK = 256
LIMIT = 2.0**40
MIB = 1024 * 1024
START = 32
WEIGHTS = 16
f32 = jnp.float32
bf16 = jnp.bfloat16
NT = (((1,), (1,)), ((), ()))
NN = (((1,), (0,)), ((), ()))


def dot(left, right, dims=NN):
    return lax.dot_general(left, right, dims, preferred_element_type=f32)


def halves(wide):
    high = wide.astype(bf16)
    return high, (wide - high.astype(f32)).astype(bf16)


def stacked(wide):
    return jnp.concatenate(halves(wide), axis=0)


def whole(shape):
    return pl.BlockSpec(shape, lambda *ids: (0,) * len(shape))


def params(mib):
    return pltpu.CompilerParams(vmem_limit_bytes=mib * MIB)


def columns_of(rows):
    return jnp.transpose(rows).astype(jnp.int32)


def stack_columns(cols, first, count):
    return jnp.concatenate([cols[:, i : i + 1] for i in range(first, first + count)], axis=0)


def attend_kernel(core, mine_ref, other_ref, kept_ref, k_any, v_any, t_ref, q2_ref, pos_ref, kk_ref, kv_ref, m_ref, acc_ref, k2_ref, v2_ref, k_buf, v_buf, sem):
    step = pl.program_id(0)
    steps = pl.num_programs(0)
    rows = q2_ref.shape[0]
    own = rows // 2
    tiles = rows // ROWS
    slots = PICK // 8
    slot = lax.rem(step, 2)

    def copies(j, to):
        here = pl.ds(pl.multiple_of(j * BLOCK, BLOCK), BLOCK)
        return (
            pltpu.make_async_copy(k_any.at[core[0], here, :], k_buf.at[to], sem.at[0, to]),
            pltpu.make_async_copy(v_any.at[core[0], here, :], v_buf.at[to], sem.at[1, to]),
        )

    def fetch(j, to):
        for copy in copies(j, to):
            copy.start()

    def arrive(j, to):
        for copy in copies(j, to):
            copy.wait()

    @pl.when(step == 0)
    def _():
        fetch(0, 0)
        for part, ref in enumerate((mine_ref.at[0], other_ref)):
            high, low = halves(ref[:own, :])
            q2_ref[pl.ds(part * own, own), :HD] = high
            q2_ref[pl.ds(part * own, own), HD:] = low
            pos_ref[pl.ds(part * own // LANES, own // LANES), :] = ref[own:, :]
        m_ref[...] = jnp.full(m_ref.shape, -jnp.inf, f32)
        acc_ref[...] = jnp.zeros(acc_ref.shape, f32)
        v2_ref[:, HD:] = jnp.ones((BLOCK, HD), bf16)

    @pl.when(step + 1 < steps)
    def _():
        fetch(step + 1, 1 - slot)

    arrive(step, slot)

    def load(of):
        k2_ref[:, :HD] = k_buf[of]
        k2_ref[:, HD:] = k_buf[of]
        v2_ref[:, :HD] = v_buf[of]

    def pick():
        per = BLOCK // 8
        kept_row = kept_ref[pl.ds(core[0], 1), pl.ds(pl.multiple_of(step * per, per), per)] - step * BLOCK
        lane = lax.broadcasted_iota(jnp.int32, (slots, PICK), 1)
        for half in range(per // LANES):
            col = jnp.transpose(jnp.broadcast_to(kept_row[:, half * LANES : (half + 1) * LANES], (LANES, LANES)))[:, :1]
            for piece in range(LANES // slots):
                at = (half * LANES + piece * slots) * 8
                hot = jnp.where(lane == col[piece * slots : (piece + 1) * slots, :] - at, 1.0, 0.0).astype(bf16)
                both = jnp.concatenate([k_buf[slot, at : at + PICK, :], v_buf[slot, at : at + PICK, :]], axis=1)
                got = dot(hot, both).astype(bf16)
                here = pl.ds(half * LANES + piece * slots, slots)
                kk_ref[here, :] = got[:, :HD]
                kv_ref[here, :] = got[:, HD:]

    def scores_of(tile, base, masked):
        scores = dot(q2_ref[pl.ds(tile * ROWS, ROWS), :], k2_ref[...], NT)
        if masked:
            cols = columns_of(pos_ref[...]) - base
            pos = stack_columns(cols, tile * ROWS // LANES, ROWS // LANES)
            lane = lax.broadcasted_iota(jnp.int32, scores.shape, 1)
            scores = jnp.where(lane <= pos, scores, -jnp.inf)
        return scores

    def tile_now(tile, base, masked, running):
        here = pl.ds(tile * ROWS, ROWS)
        scores = scores_of(tile, base, masked)
        if not running:
            expo = jnp.exp2(scores - m_ref[here, :1]).astype(bf16)
            acc_ref[here, :] += dot(expo, v2_ref[...])
            return
        old = m_ref[here, :]
        new = jnp.maximum(old, jnp.max(scores, axis=1, keepdims=True))
        m_ref[here, :] = new
        expo = jnp.exp2(scores - new[:, :1]).astype(bf16)
        fade = jnp.exp2(old - new)
        both = jnp.concatenate([fade, fade], axis=1)
        acc_ref[here, :] = acc_ref[here, :] * both + dot(expo, v2_ref[...])

    def go(masked, running):
        load(slot)
        for tile in range(tiles):
            tile_now(tile, step * BLOCK, masked, running)
        pick()

    early = step < steps // 2
    follow = (step == 0) | (core[0] == 0)
    for masked in (False, True):
        for running in (False, True):

            @pl.when((early != masked) & (follow == running))
            def _(masked=masked, running=running):
                go(masked, running)

    @pl.when((step == steps - 1) & jnp.logical_not(jnp.max(jnp.max(acc_ref[:, HD : HD + 1], axis=0, keepdims=True)) <= LIMIT))
    def _():
        m_ref[...] = jnp.full(m_ref.shape, -jnp.inf, f32)
        acc_ref[...] = jnp.zeros(acc_ref.shape, f32)

        def block(j, carry):
            fetch(j, 0)
            arrive(j, 0)
            load(0)
            for tile in range(tiles):
                tile_now(tile, j * BLOCK, True, True)
            return carry

        lax.fori_loop(0, steps, block, 0)

    @pl.when(step == steps - 1)
    def _():
        t_ref[...] = acc_ref[:, :HD] / acc_ref[:, HD:]


def attend(core, packed, other, kept, keys, values):
    own = packed.shape[1] - packed.shape[1] % LANES
    rows = 2 * own
    steps = keys.shape[1] // BLOCK
    count = kept.shape[1]
    per = BLOCK // 8
    return pl.pallas_call(
        attend_kernel,
        grid_spec=pltpu.PrefetchScalarGridSpec(
            num_scalar_prefetch=1,
            grid=(steps,),
            in_specs=[
                pl.BlockSpec((1,) + packed.shape[1:], lambda j, c: (c[0], 0, 0)),
                whole(other.shape),
                whole(kept.shape),
                pl.BlockSpec(memory_space=pltpu.HBM),
                pl.BlockSpec(memory_space=pltpu.HBM),
            ],
            out_specs=[
                whole((rows, HD)),
                whole((rows, 2 * HD)),
                whole((rows // LANES, LANES)),
                pl.BlockSpec((per, HD), lambda j, c: (j, 0)),
                pl.BlockSpec((per, HD), lambda j, c: (j, 0)),
            ],
            scratch_shapes=[
                pltpu.VMEM((rows, LANES), f32),
                pltpu.VMEM((rows, 2 * HD), f32),
                pltpu.VMEM((BLOCK, 2 * HD), bf16),
                pltpu.VMEM((BLOCK, 2 * HD), bf16),
                pltpu.VMEM((2, BLOCK, HD), bf16),
                pltpu.VMEM((2, BLOCK, HD), bf16),
                pltpu.SemaphoreType.DMA((2, 2)),
            ],
        ),
        out_shape=[
            jax.ShapeDtypeStruct((rows, HD), f32),
            jax.ShapeDtypeStruct((rows, 2 * HD), bf16),
            jax.ShapeDtypeStruct((rows // LANES, LANES), f32),
            jax.ShapeDtypeStruct((count, HD), bf16),
            jax.ShapeDtypeStruct((count, HD), bf16),
        ],
        compiler_params=params(40),
        name="attend",
    )(core, packed, other, kept, keys, values)


def put_chunks(z_ref, rows):
    for chunk in range(z_ref.shape[0]):
        z_ref[chunk] = rows[:, chunk * LANES : (chunk + 1) * LANES]


def pulled(two, expo):
    back = dot(two, expo)
    return back[:HD] + back[HD:]


def start_kernel(core, q2_ref, pos_ref, kept_ref, kk_ref, kv_ref, t_ref, e_hbm, over_ref, z_ref, e_ref, low_ref, two_ref, sem):
    keys = kk_ref[...]
    keys = jnp.concatenate([keys, keys], axis=1)
    kept = kept_ref[pl.ds(core[0], 1), :]
    cols = columns_of(pos_ref[...])
    for tile in range(e_ref.shape[0] // ROWS):
        here = pl.ds(tile * ROWS, ROWS)
        scores = dot(q2_ref[here, :], keys, NT)
        pos = stack_columns(cols, tile * ROWS // LANES, ROWS // LANES)
        scores = jnp.where(kept <= pos, scores, -jnp.inf)
        expo = jnp.exp2(scores - jnp.max(scores, axis=1, keepdims=True))
        over = 1.0 / jnp.sum(expo, axis=1, keepdims=True)
        high, low = halves(expo)
        e_ref[here, :] = high
        low_ref[here, :] = low
        pltpu.make_async_copy(e_ref.at[here, :], e_hbm.at[here, :], sem.at[tile]).start()
        gap = t_ref[here, :] - (dot(high, kv_ref[...]) + dot(low, kv_ref[...])) * over
        over_ref[:, here] = jnp.transpose(jnp.broadcast_to(over, (ROWS, LANES)))[:8, :]
        two_ref[:, here] = stacked(jnp.transpose(gap * over))
    put_chunks(z_ref, pulled(two_ref[...], e_ref[...]) + dot(two_ref[:HD, :], low_ref[...]))
    for tile in range(e_ref.shape[0] // ROWS):
        here = pl.ds(tile * ROWS, ROWS)
        pltpu.make_async_copy(e_ref.at[here, :], e_hbm.at[here, :], sem.at[tile]).wait()


def start(core, q2, pos, kept, kept_keys, kept_values, target):
    rows = q2.shape[0]
    count = kept_keys.shape[0]
    inputs = (q2, pos, kept, kept_keys, kept_values, target)
    return pl.pallas_call(
        start_kernel,
        grid_spec=pltpu.PrefetchScalarGridSpec(
            num_scalar_prefetch=1,
            grid=(1,),
            in_specs=[whole(x.shape) for x in inputs],
            out_specs=[
                pl.BlockSpec(memory_space=pltpu.HBM),
                whole((8, rows)),
                whole((count // LANES, HD, LANES)),
            ],
            scratch_shapes=[
                pltpu.VMEM((rows, count), bf16),
                pltpu.VMEM((rows, count), bf16),
                pltpu.VMEM((2 * HD, rows), bf16),
                pltpu.SemaphoreType.DMA((rows // ROWS,)),
            ],
        ),
        out_shape=[
            jax.ShapeDtypeStruct((rows, count), bf16),
            jax.ShapeDtypeStruct((8, rows), f32),
            jax.ShapeDtypeStruct((count // LANES, HD, LANES), f32),
        ],
        compiler_params=params(START),
        name="start",
    )(core, *inputs)


def load_vector(vec_ref, two_ref):
    for chunk in range(vec_ref.shape[0]):
        two_ref[:, chunk * LANES : (chunk + 1) * LANES] = stacked(vec_ref[chunk])


def tiles_of(e_hbm, e_ref, sem):
    copies = []
    for tile in range(e_ref.shape[0] // ROWS):
        here = pl.ds(tile * ROWS, ROWS)
        copies.append((here, pltpu.make_async_copy(e_hbm.at[here, :], e_ref.at[here, :], sem.at[tile])))
    for _, copy in copies:
        copy.start()
    return copies


def pushed(vec_ref, here, e_ref):
    two = dot(vec_ref[...], e_ref[here, :], NT)
    return two[:HD] + two[HD:]


def normal_kernel(vec_ref, over_ref, e_hbm, z_ref, two_ref, e_ref, sem, image_ref):
    copies = tiles_of(e_hbm, e_ref, sem)
    load_vector(vec_ref, two_ref)
    for here, copy in copies:
        copy.wait()
        over = over_ref[:1, here]
        image_ref[:, here] = stacked(pushed(two_ref, here, e_ref) * (over * over))
    put_chunks(z_ref, pulled(image_ref[...], e_ref[...]))


def square_kernel(vec_ref, over_ref, e_hbm, sums_ref, s_ref, two_ref, e_ref, sem):
    copies = tiles_of(e_hbm, e_ref, sem)
    load_vector(vec_ref, two_ref)
    total = jnp.zeros((1, ROWS), f32)
    for here, copy in copies:
        copy.wait()
        image = pushed(two_ref, here, e_ref) * over_ref[:1, here]
        total += jnp.sum(image * image, axis=0, keepdims=True)
    last = sum(total[:, i * LANES : (i + 1) * LANES] for i in range(ROWS // LANES))
    row = lax.broadcasted_iota(jnp.int32, sums_ref.shape, 0)
    lane = lax.broadcasted_iota(jnp.int32, sums_ref.shape, 1)
    sums = jnp.sum(jnp.where(row == 3, last, sums_ref[...]), axis=1, keepdims=True)
    line = jnp.sum(jnp.where(row == lane, sums, 0.0), axis=0, keepdims=True)
    s_ref[...] = jnp.broadcast_to(line[None], s_ref.shape)


def with_weights(kernel, name, out, vec, over, expo, *more, scratch=()):
    rows, count = expo.shape
    return pl.pallas_call(
        kernel,
        in_specs=[whole(vec.shape), whole(over.shape), pl.BlockSpec(memory_space=pltpu.HBM)] + [whole(a.shape) for a in more],
        out_specs=whole(out),
        out_shape=jax.ShapeDtypeStruct(out, f32),
        scratch_shapes=[
            pltpu.VMEM((2 * HD, count), bf16),
            pltpu.VMEM((rows, count), bf16),
            pltpu.SemaphoreType.DMA((rows // ROWS,)),
            *scratch,
        ],
        compiler_params=params(WEIGHTS),
        name=name,
    )(vec, over, expo, *more)


def fold_kernel(parts_ref, chunk_ref, copies_ref):
    total = jnp.sum(parts_ref[...], axis=0)
    chunk_ref[...] = total
    copies_ref[...] = jnp.broadcast_to(total[None], copies_ref.shape)


def fold(parts):
    return pl.pallas_call(
        fold_kernel,
        in_specs=[whole(parts.shape)],
        out_specs=[whole(parts.shape[1:]), whole(parts.shape)],
        out_shape=[jax.ShapeDtypeStruct(parts.shape[1:], f32), jax.ShapeDtypeStruct(parts.shape, f32)],
        compiler_params=params(8),
        name="fold",
    )(parts)


def fold_image_kernel(ridge, core, parts_ref, res_ref, copies_ref, sums_ref, keep_ref, send_ref, turn_ref):
    res = res_ref[...]
    total = jnp.sum(parts_ref[...], axis=0) + ridge * res
    copies_ref[...] = jnp.broadcast_to(total[None], copies_ref.shape)
    sums_ref[...] = jnp.zeros(sums_ref.shape, f32)
    sums_ref[0:1, :] = jnp.sum(res * res, axis=0, keepdims=True)
    sums_ref[1:2, :] = jnp.sum(res * total, axis=0, keepdims=True)
    sums_ref[2:3, :] = jnp.sum(total * total, axis=0, keepdims=True)
    half = keep_ref.shape[1]
    for i, chunk in enumerate((res, total)):
        turn_ref[...] = jnp.transpose(chunk)
        keep_ref[i] = turn_ref[pl.ds(pl.multiple_of(core[0] * half, half), half), :]
        send_ref[i] = turn_ref[pl.ds(pl.multiple_of((1 - core[0]) * half, half), half), :]


def fold_image(core, ridge, parts, res):
    half = (2, parts.shape[2] // 2, HD)
    return pl.pallas_call(
        lambda *refs: fold_image_kernel(ridge, *refs),
        grid_spec=pltpu.PrefetchScalarGridSpec(
            num_scalar_prefetch=1,
            grid=(1,),
            in_specs=[whole(parts.shape), whole(res.shape)],
            out_specs=[whole(parts.shape), whole((8, LANES)), whole(half), whole(half)],
            scratch_shapes=[pltpu.VMEM(res.shape, f32)],
        ),
        out_shape=[
            jax.ShapeDtypeStruct(parts.shape, f32),
            jax.ShapeDtypeStruct((8, LANES), f32),
            jax.ShapeDtypeStruct(half, f32),
            jax.ShapeDtypeStruct(half, f32),
        ],
        compiler_params=params(8),
        name="fold_image",
    )(core, parts, res)


def finish_kernel(ridge, core, sums_ref, keep_ref, got_ref, out_ref):
    sums = jnp.sum(sums_ref[...], axis=0)
    lane = lax.broadcasted_iota(jnp.int32, sums.shape, 1)
    rr, rn, nn, ww = (jnp.sum(jnp.where(lane == i, sums, 0.0), axis=1, keepdims=True) for i in range(4))
    alpha = rr / rn
    new = rr - 2.0 * alpha * rn + alpha * alpha * nn
    beta = new / rr
    grow = 1.0 + beta
    curve = grow * grow * rn - 2.0 * alpha * grow * nn + alpha * alpha * (ww + ridge * nn)
    step = new / curve
    left = alpha + step * grow
    right = -step * alpha
    out_ref[core[0]] = left * keep_ref[0] + right * keep_ref[1]
    out_ref[1 - core[0]] = left * got_ref[0] + right * got_ref[1]


def finish(core, ridge, sums, keep, got):
    return pl.pallas_call(
        lambda *refs: finish_kernel(ridge, *refs),
        grid_spec=pltpu.PrefetchScalarGridSpec(
            num_scalar_prefetch=1,
            grid=(1,),
            in_specs=[whole(sums.shape), whole(keep.shape), whole(got.shape)],
            out_specs=whole(keep.shape),
        ),
        out_shape=jax.ShapeDtypeStruct(keep.shape, f32),
        compiler_params=params(4),
        name="finish",
    )(core, sums, keep, got)


def local(history_keys, history_values, queries, positions, kept_index):
    count = kept_index.shape[1]
    own_rows = queries.shape[1]
    devices = lax.axis_size(("chip", "core"))
    everyone = lax.axis_size("head") * devices
    ridge = own_rows * devices / (count * count)
    index = lax.axis_index("core")
    core = index.astype(jnp.int32).reshape(1)
    swap = [(0, 1), (1, 0)]

    scaled = queries.astype(f32) * (math.log2(math.e) / math.sqrt(HD))
    packed = jnp.concatenate([scaled, positions.astype(f32).reshape(2, own_rows // LANES, LANES)], axis=1)
    other = lax.ppermute(lax.dynamic_index_in_dim(packed, 1 - index, 0, keepdims=False), "core", swap)
    history_keys = pltpu.with_memory_space_constraint(history_keys, pltpu.HBM)
    history_values = pltpu.with_memory_space_constraint(history_values, pltpu.HBM)
    target, q2, pos, kept_keys, kept_values = attend(core, packed, other, kept_index, history_keys, history_values)
    expo, over, z = start(core, q2, pos, kept_index, kept_keys, kept_values, target)

    def exchange(chunks):
        return lax.all_to_all(chunks, "chip", 0, 0, tiled=True)

    res, copies = fold(exchange(z))
    z = with_weights(
        normal_kernel, "normal", z.shape, exchange(copies), over, expo, scratch=[pltpu.VMEM((2 * HD, 2 * own_rows), bf16)]
    )
    copies, sums, keep, send = fold_image(core, ridge, exchange(z), res)
    copies, send = lax.optimization_barrier((exchange(copies), send))
    got = lax.ppermute(send, "core", swap)
    sums = with_weights(square_kernel, "square", (everyone, 1, LANES), copies, over, expo, sums)
    sums = lax.all_to_all(sums, ("head", "chip", "core"), 0, 0, tiled=True)
    return finish(core, ridge, sums, keep, got)


def solution(mesh):
    heads, probes = mesh.devices.shape
    split = Mesh(mesh.devices.reshape(heads, probes // 2, 2), ("head", "chip", "core"))
    probe = ("chip", "core")
    return jax.shard_map(
        local,
        mesh=split,
        in_specs=(
            P("head", None, None),
            P("head", None, None),
            P("head", probe, None),
            P("head", probe),
            P("head", None),
        ),
        out_specs=P("head", probe, None),
        check_vma=False,
    )
```

time: 227 us -> 170 us (0.75); the launches traced: 224 us -> 170 us
  starting transfers between devices: 21.1 us -> 1.5 us
  Pallas kernels: 61.4 us -> 42.7 us
  waiting for transfers between devices: 19 us -> 1.13 us
  blocking collectives: 117 us -> 122 us
    all_to_all x2 -> x0, waiting for transfers between devices: 18.7 us -> none  [the longest x1 9.4 us: local(): sums = lax.all_to_all(sums, ('head', 'probe'), 0, 0, tiled=True)]
    all_to_all x2 -> x0, starting transfers between devices: 15.4 us -> none  [the longest x1 11.8 us: local(): sums = lax.all_to_all(sums, ('head', 'probe'), 0, 0, tiled=True)]
    pallas_call x1, Pallas kernels: 30.5 us -> 24.3 us  [attend(): pl.pallas_call(attend_kernel, grid_spec=pltpu.PrefetchScalarGridSpec(num_...]
    all_to_all x3 -> x5, blocking collectives: 117 us -> 122 us  [the longest x4 108 us: exchange(): return lax.all_to_all(chunks, 'chip', 0, 0, tiled=True)]
    ppermute x1, starting transfers between devices: 4.16 us -> 0.01 us  [local(): got = lax.ppermute(send, 'core', swap)]
    pallas_call x2, Pallas kernels: 12.3 us -> 8.18 us  [with_weights(): pl.pallas_call(kernel, in_specs=[whole(vec.shape), whole(over.shape), pl....]
    pallas_call x1, Pallas kernels: 12 us -> 9.07 us  [start(): pl.pallas_call(start_kernel, grid_spec=pltpu.PrefetchScalarGridSpec(num_s...]
  transfers between devices with their start and end apart: 4 -> 2, of which waited for: 3 -> 1; matrix products, arithmetic and copies ran while one was open for 0% -> 0% of each run, Pallas kernels for 2% -> 2%
where the time goes in v3:
time: 170 us
  blocking collectives  122 us (72%)
  Pallas kernels  42.7 us (25%)
  other arithmetic  1.74 us (1%)
    all_to_all x4, blocking collectives, exchange(): return lax.all_to_all(chunks, 'chip', 0, 0, tiled=True)  108 us
    pallas_call x1, Pallas kernels, attend(): pl.pallas_call(attend_kernel, grid_spec=pltpu.PrefetchScalarGridSpec(num_...  24.3 us
    all_to_all x1, blocking collectives, local(): sums = lax.all_to_all(sums, ('head', 'chip', 'core'), 0, 0, tiled=True)  14.5 us
    pallas_call x1, Pallas kernels, start(): pl.pallas_call(start_kernel, grid_spec=pltpu.PrefetchScalarGridSpec(num_s...  9.07 us
    pallas_call x2, Pallas kernels, with_weights(): pl.pallas_call(kernel, in_specs=[whole(vec.shape), whole(over.shape), pl....  8.18 us
  transfers between devices with their start and end apart: 2, of which 1 were waited for; matrix products, arithmetic and copies ran while one was open for 0% of the time, Pallas kernels for 2%

profile of v3, /device:TPU:1, one launch (start us, length us, event | category | flops | bytes accessed | tf_op | source)
XLA Modules:
  0.0 169.9 jit_solution(8948751833437345562)
XLA Ops:
  0.0 0.7 convert_element_type.7
  0.7 1.0 convert_multiply_fusion
  1.7 1.5 collective-permute-start
  3.3 1.1 collective-permute-done.other_ref
  4.4 0.0 copy-start
  4.4 0.7 copy-done
  5.1 24.3 %attend.1 = (f32[1024,128]{1,0:T(8,128)S(1)}, bf16[1024,256]{1,0:T(8,128)(2,1)S(1)}, f32[8,128]{1,0:T(8,128)S(1)}, bf16[2048,128]{1,0:T(8,128)(2,1)S(1)}, bf16[2048,128]{1,0:T(8,128)(2,1)S(1)}) custom-call(s32[1]{0:T(128)} %bitcast.core.refs_0_, f32[2,516,128]{2,1,0:T(8,128)S(1)} %pad_maximum_fusion.mine_ref, f32[516,128]{1,0:T(8,128)S(1)} %collective-permute-done.other_ref, ...), custom_call_target="tpu_custom_call" | custom-call | tf_op jit(solution)/shard_map/attend/pallas_call | solution.py:182
  29.4 9.1 %start.1 = (bf16[1024,2048]{1,0:T(8,128)(2,1)S(1)}, f32[8,1024]{1,0:T(8,128)S(1)}, f32[16,128,128]{2,1,0:T(8,128)S(1)}) custom-call(s32[1]{0:T(128)} %bitcast.core.refs_0_, bf16[1024,256]{1,0:T(8,128)(2,1)S(1)} %get-tuple-element.21.q2_ref, f32[8,128]{1,0:T(8,128)S(1)} %get-tuple-element.22.pos_ref, s32[2,2048]{1,0:T(2,128)S(1)} %copy-done, ...), custom_call_target="tpu_custom_call" | custom-call | tf_op jit(solution)/shard_map/start/pallas_call | solution.py:262
  38.5 62.4 %all_to_all.25.parts_ref = f32[16,128,128]{2,1,0:T(8,128)S(1)} all-to-all(f32[16,128,128]{2,1,0:T(8,128)S(1)} %get-tuple-element.26), channel_id=1, replica_groups=mesh['head'=4,'chip'=16,'core'=2] {'chip'}, dimensions={0} | all-to-all | bytes 2097152 | tf_op jit(solution)/shard_map/all_to_all | solution.py:458
  100.8 0.1 fold.1
  101.0 16.0 %all_to_all.26.vec_ref = f32[16,128,128]{2,1,0:T(8,128)S(1)} all-to-all(f32[16,128,128]{2,1,0:T(8,128)S(1)} %get-tuple-element.27), channel_id=1, replica_groups=mesh['head'=4,'chip'=16,'core'=2] {'chip'}, dimensions={0} | all-to-all | bytes 2097152 | tf_op jit(solution)/shard_map/all_to_all | solution.py:458
  117.0 4.6 %normal.1 = f32[16,128,128]{2,1,0:T(8,128)S(1)} custom-call(f32[16,128,128]{2,1,0:T(8,128)S(1)} %all_to_all.26.vec_ref, f32[8,1024]{1,0:T(8,128)S(1)} %get-tuple-element.28.over_ref, bf16[1024,2048]{1,0:T(8,128)(2,1)S(1)} %get-tuple-element.29.e_hbm), custom_call_target="tpu_custom_call" | custom-call | tf_op jit(solution)/shard_map/normal/pallas_call | solution.py:338
  121.6 14.7 %all_to_all.27.refs_1_ = f32[16,128,128]{2,1,0:T(8,128)S(1)} all-to-all(f32[16,128,128]{2,1,0:T(8,128)S(1)} %normal.1), channel_id=1, replica_groups=mesh['head'=4,'chip'=16,'core'=2] {'chip'}, dimensions={0} | all-to-all | bytes 2097152 | tf_op jit(solution)/shard_map/all_to_all | solution.py:458
  136.3 0.2 fold_image.1
  136.5 14.5 %all_to_all.28.vec_ref = f32[16,128,128]{2,1,0:T(8,128)S(1)} all-to-all(f32[16,128,128]{2,1,0:T(8,128)S(1)} %get-tuple-element.31), channel_id=1, replica_groups=mesh['head'=4,'chip'=16,'core'=2] {'chip'}, dimensions={0} | all-to-all | bytes 2097152 | tf_op jit(solution)/shard_map/all_to_all | solution.py:458
  151.0 0.0 collective-permute-start.1
  151.0 3.6 %square.1 = f32[128,1,128]{2,1,0:T(1,128)S(1)} custom-call(f32[16,128,128]{2,1,0:T(8,128)S(1)} %all_to_all.28.vec_ref, f32[8,1024]{1,0:T(8,128)S(1)} %get-tuple-element.28.over_ref, bf16[1024,2048]{1,0:T(8,128)(2,1)S(1)} %get-tuple-element.29.e_hbm, f32[8,128]{1,0:T(8,128)S(1)} %get-tuple-element.34.sums_ref), custom_call_target="tpu_custom_call" | custom-call | tf_op jit(solution)/shard_map/square/pallas_call | solution.py:338
  154.6 14.5 %all_to_all.29.refs_1_ = f32[128,1,128]{2,1,0:T(1,128)S(1)} all-to-all(f32[128,1,128]{2,1,0:T(1,128)S(1)} %square.1), channel_id=1, replica_groups=mesh['head'=4,'chip'=16,'core'=2] {'head','chip','core'}, dimensions={0} | all-to-all | bytes 131072 | tf_op jit(solution)/shard_map/all_to_all | solution.py:468
  169.0 0.0 collective-permute-done.1.refs_3_
  169.0 0.9 finish.1
  (3 shorter events, 0.1 us)
Async XLA Ops:
  1.7 2.7 %collective-permute-start = (f32[516,128]{1,0:T(8,128)S(1)}, f32[516,128]{1,0:T(8,128)S(1)}, u32[]{:S(2)}, u32[]{:S(2)}) collective-permute-start(f32[516,128]{1,0:T(8,128)S(1)} %fusion.1), channel_id=1, source_target_pairs={{0,1},{1,0},{2,3},{3,2},{4,5},{5,4},{6,7},{7,6},{8,9},{9,8},{10,11... | collective-permute-start | bytes 792584 | tf_op jit(solution)/shard_map/ppermute | solution.py:451
  4.4 0.7 copy-start
  151.0 18.1 %collective-permute-start.1 = (f32[2,64,128]{2,1,0:T(8,128)S(1)}, f32[2,64,128]{2,1,0:T(8,128)S(1)}, u32[]{:S(2)}, u32[]{:S(2)}) collective-permute-start(f32[2,64,128]{2,1,0:T(8,128)S(1)} %get-tuple-element.36), channel_id=1, source_target_pairs={{0,1},{1,0},{2,3},{3,2},{4,5},{5,4},{6,7},{7,6},{8,9},{9,8},{10,11... | collective-permute-start | bytes 196616 | tf_op jit(solution)/shard_map/ppermute | solution.py:466

commit v4 on v3

--- a/solution.py
+++ b/solution.py
@@ -14,6 +14,7 @@
 ROWS = 256
 PICK = 256
 LIMIT = 2.0**40
+SCALE = math.log2(math.e) / math.sqrt(HD)
 MIB = 1024 * 1024
 START = 32
 WEIGHTS = 16
@@ -52,11 +53,43 @@
     return jnp.concatenate([cols[:, i : i + 1] for i in range(first, first + count)], axis=0)
 
 
-def attend_kernel(core, mine_ref, other_ref, kept_ref, k_any, v_any, t_ref, q2_ref, pos_ref, kk_ref, kv_ref, m_ref, acc_ref, k2_ref, v2_ref, k_buf, v_buf, sem):
+def row_of(ref, which, here):
+    return jnp.where(which == 0, ref[0:1, here], ref[1:2, here])
+
+
+def pack_kernel(core, q_ref, place_ref, out_ref):
+    own = q_ref.shape[1]
+    out_ref[:own, :] = q_ref[1 - core[0]].astype(f32)
+    for line in range(own // LANES):
+        here = pl.ds(line * LANES, LANES)
+        out_ref[own + line : own + line + 1, :] = row_of(place_ref, 1 - core[0], here).astype(f32)
+    out_ref[own + own // LANES :, :] = jnp.zeros((8 - own // LANES % 8, LANES), f32)
+
+
+def pack(core, queries, positions):
+    own = queries.shape[1]
+    lines = own // LANES
+    out = (own + lines + 8 - lines % 8, HD)
+    return pl.pallas_call(
+        pack_kernel,
+        grid_spec=pltpu.PrefetchScalarGridSpec(
+            num_scalar_prefetch=1,
+            grid=(1,),
+            in_specs=[whole(queries.shape), whole(positions.shape)],
+            out_specs=whole(out),
+        ),
+        out_shape=jax.ShapeDtypeStruct(out, f32),
+        compiler_params=params(4),
+        name="pack",
+    )(core, queries, positions)
+
+
+def attend_kernel(core, mine_ref, place_ref, other_ref, kept_ref, k_any, v_any, t_ref, q_ref, pos_ref, kk_ref, kv_ref, m_ref, acc_ref, v2_ref, k_buf, v_buf, sem):
     step = pl.program_id(0)
     steps = pl.num_programs(0)
-    rows = q2_ref.shape[0]
+    rows = q_ref.shape[0]
     own = rows // 2
+    lines = own // LANES
     tiles = rows // ROWS
     slots = PICK // 8
     slot = lax.rem(step, 2)
@@ -79,11 +112,12 @@
     @pl.when(step == 0)
     def _():
         fetch(0, 0)
-        for part, ref in enumerate((mine_ref.at[0], other_ref)):
-            high, low = halves(ref[:own, :])
-            q2_ref[pl.ds(part * own, own), :HD] = high
-            q2_ref[pl.ds(part * own, own), HD:] = low
-            pos_ref[pl.ds(part * own // LANES, own // LANES), :] = ref[own:, :]
+        q_ref[:own, :] = mine_ref[core[0]]
+        q_ref[own:, :] = other_ref[:own, :].astype(bf16)
+        for line in range(lines):
+            here = pl.ds(line * LANES, LANES)
+            pos_ref[line : line + 1, :] = row_of(place_ref, core[0], here).astype(f32)
+        pos_ref[lines:, :] = other_ref[own : own + lines, :]
         m_ref[...] = jnp.full(m_ref.shape, -jnp.inf, f32)
         acc_ref[...] = jnp.zeros(acc_ref.shape, f32)
         v2_ref[:, HD:] = jnp.ones((BLOCK, HD), bf16)
@@ -95,8 +129,6 @@
     arrive(step, slot)
 
     def load(of):
-        k2_ref[:, :HD] = k_buf[of]
-        k2_ref[:, HD:] = k_buf[of]
         v2_ref[:, :HD] = v_buf[of]
 
     def pick():
@@ -114,8 +146,8 @@
                 kk_ref[here, :] = got[:, :HD]
                 kv_ref[here, :] = got[:, HD:]
 
-    def scores_of(tile, base, masked):
-        scores = dot(q2_ref[pl.ds(tile * ROWS, ROWS), :], k2_ref[...], NT)
+    def scores_of(tile, of, base, masked):
+        scores = dot(q_ref[pl.ds(tile * ROWS, ROWS), :], k_buf[of], NT) * SCALE
         if masked:
             cols = columns_of(pos_ref[...]) - base
             pos = stack_columns(cols, tile * ROWS // LANES, ROWS // LANES)
@@ -123,9 +155,9 @@
             scores = jnp.where(lane <= pos, scores, -jnp.inf)
         return scores
 
-    def tile_now(tile, base, masked, running):
+    def tile_now(tile, of, base, masked, running):
         here = pl.ds(tile * ROWS, ROWS)
-        scores = scores_of(tile, base, masked)
+        scores = scores_of(tile, of, base, masked)
         if not running:
             expo = jnp.exp2(scores - m_ref[here, :1]).astype(bf16)
             acc_ref[here, :] += dot(expo, v2_ref[...])
@@ -141,11 +173,11 @@
     def go(masked, running):
         load(slot)
         for tile in range(tiles):
-            tile_now(tile, step * BLOCK, masked, running)
+            tile_now(tile, slot, step * BLOCK, masked, running)
         pick()
 
     early = step < steps // 2
-    follow = (step == 0) | (core[0] == 0)
+    follow = (step == 0) | ((core[0] == 0) & (step >= steps // 2))
     for masked in (False, True):
         for running in (False, True):
 
@@ -163,7 +195,7 @@
             arrive(j, 0)
             load(0)
             for tile in range(tiles):
-                tile_now(tile, j * BLOCK, True, True)
+                tile_now(tile, 0, j * BLOCK, True, True)
             return carry
 
         lax.fori_loop(0, steps, block, 0)
@@ -173,9 +205,8 @@
         t_ref[...] = acc_ref[:, :HD] / acc_ref[:, HD:]
 
 
-def attend(core, packed, other, kept, keys, values):
-    own = packed.shape[1] - packed.shape[1] % LANES
-    rows = 2 * own
+def attend(core, queries, positions, other, kept, keys, values):
+    rows = 2 * queries.shape[1]
     steps = keys.shape[1] // BLOCK
     count = kept.shape[1]
     per = BLOCK // 8
@@ -185,7 +216,8 @@
             num_scalar_prefetch=1,
             grid=(steps,),
             in_specs=[
-                pl.BlockSpec((1,) + packed.shape[1:], lambda j, c: (c[0], 0, 0)),
+                whole(queries.shape),
+                whole(positions.shape),
                 whole(other.shape),
                 whole(kept.shape),
                 pl.BlockSpec(memory_space=pltpu.HBM),
@@ -193,7 +225,7 @@
             ],
             out_specs=[
                 whole((rows, HD)),
-                whole((rows, 2 * HD)),
+                whole((rows, HD)),
                 whole((rows // LANES, LANES)),
                 pl.BlockSpec((per, HD), lambda j, c: (j, 0)),
                 pl.BlockSpec((per, HD), lambda j, c: (j, 0)),
@@ -202,7 +234,6 @@
                 pltpu.VMEM((rows, LANES), f32),
                 pltpu.VMEM((rows, 2 * HD), f32),
                 pltpu.VMEM((BLOCK, 2 * HD), bf16),
-                pltpu.VMEM((BLOCK, 2 * HD), bf16),
                 pltpu.VMEM((2, BLOCK, HD), bf16),
                 pltpu.VMEM((2, BLOCK, HD), bf16),
                 pltpu.SemaphoreType.DMA((2, 2)),
@@ -210,14 +241,14 @@
         ),
         out_shape=[
             jax.ShapeDtypeStruct((rows, HD), f32),
-            jax.ShapeDtypeStruct((rows, 2 * HD), bf16),
+            jax.ShapeDtypeStruct((rows, HD), bf16),
             jax.ShapeDtypeStruct((rows // LANES, LANES), f32),
             jax.ShapeDtypeStruct((count, HD), bf16),
             jax.ShapeDtypeStruct((count, HD), bf16),
         ],
         compiler_params=params(40),
         name="attend",
-    )(core, packed, other, kept, keys, values)
+    )(core, queries, positions, other, kept, keys, values)
 
 
 def put_chunks(z_ref, rows):
@@ -230,14 +261,12 @@
     return back[:HD] + back[HD:]
 
 
-def start_kernel(core, q2_ref, pos_ref, kept_ref, kk_ref, kv_ref, t_ref, e_hbm, over_ref, z_ref, e_ref, low_ref, two_ref, sem):
-    keys = kk_ref[...]
-    keys = jnp.concatenate([keys, keys], axis=1)
+def start_kernel(core, q_ref, pos_ref, kept_ref, kk_ref, kv_ref, t_ref, e_ref, over_ref, z_ref, low_ref, two_ref):
     kept = kept_ref[pl.ds(core[0], 1), :]
     cols = columns_of(pos_ref[...])
     for tile in range(e_ref.shape[0] // ROWS):
         here = pl.ds(tile * ROWS, ROWS)
-        scores = dot(q2_ref[here, :], keys, NT)
+        scores = dot(q_ref[here, :], kk_ref[...], NT) * SCALE
         pos = stack_columns(cols, tile * ROWS // LANES, ROWS // LANES)
         scores = jnp.where(kept <= pos, scores, -jnp.inf)
         expo = jnp.exp2(scores - jnp.max(scores, axis=1, keepdims=True))
@@ -245,20 +274,16 @@
         high, low = halves(expo)
         e_ref[here, :] = high
         low_ref[here, :] = low
-        pltpu.make_async_copy(e_ref.at[here, :], e_hbm.at[here, :], sem.at[tile]).start()
         gap = t_ref[here, :] - (dot(high, kv_ref[...]) + dot(low, kv_ref[...])) * over
         over_ref[:, here] = jnp.transpose(jnp.broadcast_to(over, (ROWS, LANES)))[:8, :]
         two_ref[:, here] = stacked(jnp.transpose(gap * over))
     put_chunks(z_ref, pulled(two_ref[...], e_ref[...]) + dot(two_ref[:HD, :], low_ref[...]))
-    for tile in range(e_ref.shape[0] // ROWS):
-        here = pl.ds(tile * ROWS, ROWS)
-        pltpu.make_async_copy(e_ref.at[here, :], e_hbm.at[here, :], sem.at[tile]).wait()
-
-
-def start(core, q2, pos, kept, kept_keys, kept_values, target):
-    rows = q2.shape[0]
+
+
+def start(core, q, pos, kept, kept_keys, kept_values, target):
+    rows = q.shape[0]
     count = kept_keys.shape[0]
-    inputs = (q2, pos, kept, kept_keys, kept_values, target)
+    inputs = (q, pos, kept, kept_keys, kept_values, target)
     return pl.pallas_call(
         start_kernel,
         grid_spec=pltpu.PrefetchScalarGridSpec(
@@ -266,15 +291,13 @@
             grid=(1,),
             in_specs=[whole(x.shape) for x in inputs],
             out_specs=[
-                pl.BlockSpec(memory_space=pltpu.HBM),
+                whole((rows, count)),
                 whole((8, rows)),
                 whole((count // LANES, HD, LANES)),
             ],
             scratch_shapes=[
                 pltpu.VMEM((rows, count), bf16),
-                pltpu.VMEM((rows, count), bf16),
                 pltpu.VMEM((2 * HD, rows), bf16),
-                pltpu.SemaphoreType.DMA((rows // ROWS,)),
             ],
         ),
         out_shape=[
@@ -292,14 +315,8 @@
         two_ref[:, chunk * LANES : (chunk + 1) * LANES] = stacked(vec_ref[chunk])
 
 
-def tiles_of(e_hbm, e_ref, sem):
-    copies = []
-    for tile in range(e_ref.shape[0] // ROWS):
-        here = pl.ds(tile * ROWS, ROWS)
-        copies.append((here, pltpu.make_async_copy(e_hbm.at[here, :], e_ref.at[here, :], sem.at[tile])))
-    for _, copy in copies:
-        copy.start()
-    return copies
+def tiles_of(e_ref):
+    return [pl.ds(tile * ROWS, ROWS) for tile in range(e_ref.shape[0] // ROWS)]
 
 
 def pushed(vec_ref, here, e_ref):
@@ -307,22 +324,18 @@
     return two[:HD] + two[HD:]
 
 
-def normal_kernel(vec_ref, over_ref, e_hbm, z_ref, two_ref, e_ref, sem, image_ref):
-    copies = tiles_of(e_hbm, e_ref, sem)
+def normal_kernel(vec_ref, over_ref, e_ref, z_ref, two_ref, image_ref):
     load_vector(vec_ref, two_ref)
-    for here, copy in copies:
-        copy.wait()
+    for here in tiles_of(e_ref):
         over = over_ref[:1, here]
         image_ref[:, here] = stacked(pushed(two_ref, here, e_ref) * (over * over))
     put_chunks(z_ref, pulled(image_ref[...], e_ref[...]))
 
 
-def square_kernel(vec_ref, over_ref, e_hbm, sums_ref, s_ref, two_ref, e_ref, sem):
-    copies = tiles_of(e_hbm, e_ref, sem)
+def square_kernel(vec_ref, over_ref, e_ref, sums_ref, s_ref, two_ref):
     load_vector(vec_ref, two_ref)
     total = jnp.zeros((1, ROWS), f32)
-    for here, copy in copies:
-        copy.wait()
+    for here in tiles_of(e_ref):
         image = pushed(two_ref, here, e_ref) * over_ref[:1, here]
         total += jnp.sum(image * image, axis=0, keepdims=True)
     last = sum(total[:, i * LANES : (i + 1) * LANES] for i in range(ROWS // LANES))
@@ -337,13 +350,11 @@
     rows, count = expo.shape
     return pl.pallas_call(
         kernel,
-        in_specs=[whole(vec.shape), whole(over.shape), pl.BlockSpec(memory_space=pltpu.HBM)] + [whole(a.shape) for a in more],
+        in_specs=[whole(vec.shape), whole(over.shape), whole(expo.shape)] + [whole(a.shape) for a in more],
         out_specs=whole(out),
         out_shape=jax.ShapeDtypeStruct(out, f32),
         scratch_shapes=[
             pltpu.VMEM((2 * HD, count), bf16),
-            pltpu.VMEM((rows, count), bf16),
-            pltpu.SemaphoreType.DMA((rows // ROWS,)),
             *scratch,
         ],
         compiler_params=params(WEIGHTS),
@@ -446,13 +457,16 @@
     core = index.astype(jnp.int32).reshape(1)
     swap = [(0, 1), (1, 0)]
 
-    scaled = queries.astype(f32) * (math.log2(math.e) / math.sqrt(HD))
-    packed = jnp.concatenate([scaled, positions.astype(f32).reshape(2, own_rows // LANES, LANES)], axis=1)
-    other = lax.ppermute(lax.dynamic_index_in_dim(packed, 1 - index, 0, keepdims=False), "core", swap)
-    history_keys = pltpu.with_memory_space_constraint(history_keys, pltpu.HBM)
-    history_values = pltpu.with_memory_space_constraint(history_values, pltpu.HBM)
-    target, q2, pos, kept_keys, kept_values = attend(core, packed, other, kept_index, history_keys, history_values)
-    expo, over, z = start(core, q2, pos, kept_index, kept_keys, kept_values, target)
+    history_keys, history_values, queries, positions, kept_index = (
+        pltpu.with_memory_space_constraint(x, pltpu.HBM)
+        for x in (history_keys, history_values, queries, positions, kept_index)
+    )
+
+    other = lax.ppermute(pack(core, queries, positions), "core", swap)
+    target, q, pos, kept_keys, kept_values = attend(
+        core, queries, positions, other, kept_index, history_keys, history_values
+    )
+    expo, over, z = start(core, q, pos, kept_index, kept_keys, kept_values, target)
 
     def exchange(chunks):
         return lax.all_to_all(chunks, "chip", 0, 0, tiled=True)

time: 170 us -> 175 us (1.029)
  Pallas kernels: 42.7 us -> 82.1 us
  blocking collectives: 122 us -> 82.9 us
  starting transfers between devices: 1.5 us -> 9.66 us
    pallas_call x1, Pallas kernels: 24.3 us -> 68 us  [attend(): pl.pallas_call(attend_kernel, grid_spec=pltpu.PrefetchScalarGridSpec(num_...]
    all_to_all x4, blocking collectives: 108 us -> 65.3 us  [exchange(): return lax.all_to_all(chunks, 'chip', 0, 0, tiled=True)]
    ppermute x1, starting transfers between devices: 0.01 us -> 8.16 us  [local(): got = lax.ppermute(send, 'core', swap)]
    pallas_call x2 -> x3, Pallas kernels: 8.18 us -> 4.83 us  [the longest x2 3.85 us: with_weights(): pl.pallas_call(kernel, in_specs=[whole(vec.shape), whole(over.shape), who...]
    all_to_all x1, blocking collectives: 14.5 us -> 17.5 us  [local(): sums = lax.all_to_all(sums, ('head', 'chip', 'core'), 0, 0, tiled=True)]
  transfers between devices with their start and end apart: 2 -> 2, of which waited for: 1 -> 1; matrix products, arithmetic and copies ran while one was open for 0% -> 0% of each run, Pallas kernels for 2% -> 1%
where the time goes in v4:
time: 175 us; the launch traced here: 176 us
  blocking collectives  82.9 us (47%)
  Pallas kernels  82.1 us (47%)
  starting transfers between devices  9.66 us (6%)
    pallas_call x1, Pallas kernels, attend(): pl.pallas_call(attend_kernel, grid_spec=pltpu.PrefetchScalarGridSpec(num_...  68 us
    all_to_all x4, blocking collectives, exchange(): return lax.all_to_all(chunks, 'chip', 0, 0, tiled=True)  65.3 us
    all_to_all x1, blocking collectives, local(): sums = lax.all_to_all(sums, ('head', 'chip', 'core'), 0, 0, tiled=True)  17.5 us
    ppermute x1, starting transfers between devices, local(): got = lax.ppermute(send, 'core', swap)  8.16 us
    pallas_call x1, Pallas kernels, start(): pl.pallas_call(start_kernel, grid_spec=pltpu.PrefetchScalarGridSpec(num_s...  8.07 us
    pallas_call x2, Pallas kernels, with_weights(): pl.pallas_call(kernel, in_specs=[whole(vec.shape), whole(over.shape), who...  3.85 us
  transfers between devices with their start and end apart: 2, of which 1 were waited for; matrix products, arithmetic and copies ran while one was open for 0% of the time, Pallas kernels for 1%

profile of v4, /device:TPU:1, one launch (start us, length us, event | category | flops | bytes accessed | tf_op | source)
XLA Modules:
  0.0 175.8 jit_solution(14473117999542792201)
XLA Ops:
  0.0 1.0 pack.1
  1.0 1.5 collective-permute-start
  2.5 1.2 collective-permute-done.other_ref
  3.6 68.0 %attend.1 = (f32[1024,128]{1,0:T(8,128)S(1)}, bf16[1024,128]{1,0:T(8,128)(2,1)S(1)}, f32[8,128]{1,0:T(8,128)S(1)}, bf16[2048,128]{1,0:T(8,128)(2,1)S(1)}, bf16[2048,128]{1,0:T(8,128)(2,1)S(1)}) custom-call(s32[1]{0:T(128)} %bitcast.core.refs_0_, bf16[2,512,128]{2,1,0:T(8,128)(2,1)} %mine_ref.1, s32[2,512]{1,0:T(2,128)} %place_ref.3, ...), custom_call_target="tpu_custom_call" | custom-call | tf_op jit(solution)/shard_map/attend/pallas_call | solution.py:213
  71.6 8.1 %start.1 = (bf16[1024,2048]{1,0:T(8,128)(2,1)S(1)}, f32[8,1024]{1,0:T(8,128)S(1)}, f32[16,128,128]{2,1,0:T(8,128)S(1)}) custom-call(s32[1]{0:T(128)} %bitcast.core.refs_0_, bf16[1024,128]{1,0:T(8,128)(2,1)S(1)} %get-tuple-element.21.q_ref, f32[8,128]{1,0:T(8,128)S(1)} %get-tuple-element.22.pos_ref, s32[2,2048]{1,0:T(2,128)} %kept_ref.3, ...), custom_call_target="tpu_custom_call" | custom-call | tf_op jit(solution)/shard_map/start/pallas_call | solution.py:287
  79.7 20.6 %all_to_all.25.parts_ref = f32[16,128,128]{2,1,0:T(8,128)S(1)} all-to-all(f32[16,128,128]{2,1,0:T(8,128)S(1)} %get-tuple-element.26), channel_id=1, replica_groups=mesh['head'=4,'chip'=16,'core'=2] {'chip'}, dimensions={0} | all-to-all | bytes 2097152 | tf_op jit(solution)/shard_map/all_to_all | solution.py:472
  100.3 0.1 fold.1
  100.5 15.6 %all_to_all.26.vec_ref = f32[16,128,128]{2,1,0:T(8,128)S(1)} all-to-all(f32[16,128,128]{2,1,0:T(8,128)S(1)} %get-tuple-element.27), channel_id=1, replica_groups=mesh['head'=4,'chip'=16,'core'=2] {'chip'}, dimensions={0} | all-to-all | bytes 2097152 | tf_op jit(solution)/shard_map/all_to_all | solution.py:472
  116.1 2.4 %normal.1 = f32[16,128,128]{2,1,0:T(8,128)S(1)} custom-call(f32[16,128,128]{2,1,0:T(8,128)S(1)} %all_to_all.26.vec_ref, f32[8,1024]{1,0:T(8,128)S(1)} %get-tuple-element.28.over_ref, bf16[1024,2048]{1,0:T(8,128)(2,1)S(1)} %get-tuple-element.29.e_ref), custom_call_target="tpu_custom_call" | custom-call | tf_op jit(solution)/shard_map/normal/pallas_call | solution.py:351
  118.5 14.6 %all_to_all.27.refs_1_ = f32[16,128,128]{2,1,0:T(8,128)S(1)} all-to-all(f32[16,128,128]{2,1,0:T(8,128)S(1)} %normal.1), channel_id=1, replica_groups=mesh['head'=4,'chip'=16,'core'=2] {'chip'}, dimensions={0} | all-to-all | bytes 2097152 | tf_op jit(solution)/shard_map/all_to_all | solution.py:472
  133.1 0.2 fold_image.1
  133.3 14.5 %all_to_all.28.vec_ref = f32[16,128,128]{2,1,0:T(8,128)S(1)} all-to-all(f32[16,128,128]{2,1,0:T(8,128)S(1)} %get-tuple-element.31), channel_id=1, replica_groups=mesh['head'=4,'chip'=16,'core'=2] {'chip'}, dimensions={0} | all-to-all | bytes 2097152 | tf_op jit(solution)/shard_map/all_to_all | solution.py:472
  147.8 8.2 %collective-permute-start.1 = (f32[2,64,128]{2,1,0:T(8,128)S(1)}, f32[2,64,128]{2,1,0:T(8,128)S(1)}, u32[]{:S(2)}, u32[]{:S(2)}) collective-permute-start(f32[2,64,128]{2,1,0:T(8,128)S(1)} %get-tuple-element.36), channel_id=1, source_target_pairs={{0,1},{1,0},{2,3},{3,2},{4,5},{5,4},{6,7},{7,6},{8,9},{9,8},{10,11... | collective-permute-start | bytes 196616 | tf_op jit(solution)/shard_map/ppermute | solution.py:480
  156.0 1.4 square.1
  157.4 17.5 %all_to_all.29.refs_1_ = f32[128,1,128]{2,1,0:T(1,128)S(1)} all-to-all(f32[128,1,128]{2,1,0:T(1,128)S(1)} %square.1), channel_id=1, replica_groups=mesh['head'=4,'chip'=16,'core'=2] {'head','chip','core'}, dimensions={0} | all-to-all | bytes 131072 | tf_op jit(solution)/shard_map/all_to_all | solution.py:482
  175.0 0.0 collective-permute-done.1.refs_3_
  175.0 0.9 finish.1
Async XLA Ops:
  1.0 2.7 %collective-permute-start = (f32[520,128]{1,0:T(8,128)S(1)}, f32[520,128]{1,0:T(8,128)S(1)}, u32[]{:S(2)}, u32[]{:S(2)}) collective-permute-start(f32[520,128]{1,0:T(8,128)S(1)} %pack.1), channel_id=1, source_target_pairs={{0,1},{1,0},{2,3},{3,2},{4,5},{5,4},{6,7},{7,6},{8,9},{9,8},{10,11... | collective-permute-start | bytes 798728 | tf_op jit(solution)/shard_map/ppermute | solution.py:465
  147.8 27.1 %collective-permute-start.1 = (f32[2,64,128]{2,1,0:T(8,128)S(1)}, f32[2,64,128]{2,1,0:T(8,128)S(1)}, u32[]{:S(2)}, u32[]{:S(2)}) collective-permute-start(f32[2,64,128]{2,1,0:T(8,128)S(1)} %get-tuple-element.36), channel_id=1, source_target_pairs={{0,1},{1,0},{2,3},{3,2},{4,5},{5,4},{6,7},{7,6},{8,9},{9,8},{10,11... | collective-permute-start | bytes 196616 | tf_op jit(solution)/shard_map/ppermute | solution.py:480

commit v5 on v4

--- a/solution.py
+++ b/solution.py
@@ -57,16 +57,19 @@
     return jnp.where(which == 0, ref[0:1, here], ref[1:2, here])
 
 
-def pack_kernel(core, q_ref, place_ref, out_ref):
+def pack_kernel(core, q_ref, place_ref, kept_ref, mine_ref, send_ref, kept_out):
     own = q_ref.shape[1]
-    out_ref[:own, :] = q_ref[1 - core[0]].astype(f32)
-    for line in range(own // LANES):
-        here = pl.ds(line * LANES, LANES)
-        out_ref[own + line : own + line + 1, :] = row_of(place_ref, 1 - core[0], here).astype(f32)
-    out_ref[own + own // LANES :, :] = jnp.zeros((8 - own // LANES % 8, LANES), f32)
-
-
-def pack(core, queries, positions):
+    lines = own // LANES
+    for which, out_ref in ((core[0], mine_ref), (1 - core[0], send_ref)):
+        out_ref[:own, :] = q_ref[which].astype(f32)
+        for line in range(lines):
+            here = pl.ds(line * LANES, LANES)
+            out_ref[own + line : own + line + 1, :] = row_of(place_ref, which, here).astype(f32)
+        out_ref[own + lines :, :] = jnp.zeros((8 - lines % 8, LANES), f32)
+    kept_out[...] = kept_ref[...]
+
+
+def pack(core, queries, positions, kept):
     own = queries.shape[1]
     lines = own // LANES
     out = (own + lines + 8 - lines % 8, HD)
@@ -75,16 +78,20 @@
         grid_spec=pltpu.PrefetchScalarGridSpec(
             num_scalar_prefetch=1,
             grid=(1,),
-            in_specs=[whole(queries.shape), whole(positions.shape)],
-            out_specs=whole(out),
+            in_specs=[whole(queries.shape), whole(positions.shape), whole(kept.shape)],
+            out_specs=[whole(out), whole(out), whole(kept.shape)],
         ),
-        out_shape=jax.ShapeDtypeStruct(out, f32),
+        out_shape=[
+            jax.ShapeDtypeStruct(out, f32),
+            jax.ShapeDtypeStruct(out, f32),
+            jax.ShapeDtypeStruct(kept.shape, jnp.int32),
+        ],
         compiler_params=params(4),
         name="pack",
-    )(core, queries, positions)
-
-
-def attend_kernel(core, mine_ref, place_ref, other_ref, kept_ref, k_any, v_any, t_ref, q_ref, pos_ref, kk_ref, kv_ref, m_ref, acc_ref, v2_ref, k_buf, v_buf, sem):
+    )(core, queries, positions, kept)
+
+
+def attend_kernel(core, mine_ref, other_ref, kept_ref, k_any, v_any, t_ref, q_ref, pos_ref, kk_ref, kv_ref, m_ref, acc_ref, v2_ref, k_buf, v_buf, sem):
     step = pl.program_id(0)
     steps = pl.num_programs(0)
     rows = q_ref.shape[0]
@@ -112,12 +119,9 @@
     @pl.when(step == 0)
     def _():
         fetch(0, 0)
-        q_ref[:own, :] = mine_ref[core[0]]
-        q_ref[own:, :] = other_ref[:own, :].astype(bf16)
-        for line in range(lines):
-            here = pl.ds(line * LANES, LANES)
-            pos_ref[line : line + 1, :] = row_of(place_ref, core[0], here).astype(f32)
-        pos_ref[lines:, :] = other_ref[own : own + lines, :]
+        for part, ref in enumerate((mine_ref, other_ref)):
+            q_ref[pl.ds(part * own, own), :] = ref[:own, :].astype(bf16)
+            pos_ref[pl.ds(part * lines, lines), :] = ref[own : own + lines, :]
         m_ref[...] = jnp.full(m_ref.shape, -jnp.inf, f32)
         acc_ref[...] = jnp.zeros(acc_ref.shape, f32)
         v2_ref[:, HD:] = jnp.ones((BLOCK, HD), bf16)
@@ -205,8 +209,8 @@
         t_ref[...] = acc_ref[:, :HD] / acc_ref[:, HD:]
 
 
-def attend(core, queries, positions, other, kept, keys, values):
-    rows = 2 * queries.shape[1]
+def attend(core, mine, other, kept, keys, values):
+    rows = 2 * (mine.shape[0] // LANES * LANES)
     steps = keys.shape[1] // BLOCK
     count = kept.shape[1]
     per = BLOCK // 8
@@ -216,8 +220,7 @@
             num_scalar_prefetch=1,
             grid=(steps,),
             in_specs=[
-                whole(queries.shape),
-                whole(positions.shape),
+                whole(mine.shape),
                 whole(other.shape),
                 whole(kept.shape),
                 pl.BlockSpec(memory_space=pltpu.HBM),
@@ -248,7 +251,7 @@
         ],
         compiler_params=params(40),
         name="attend",
-    )(core, queries, positions, other, kept, keys, values)
+    )(core, mine, other, kept, keys, values)
 
 
 def put_chunks(z_ref, rows):
@@ -462,11 +465,10 @@
         for x in (history_keys, history_values, queries, positions, kept_index)
     )
 
-    other = lax.ppermute(pack(core, queries, positions), "core", swap)
-    target, q, pos, kept_keys, kept_values = attend(
-        core, queries, positions, other, kept_index, history_keys, history_values
-    )
-    expo, over, z = start(core, q, pos, kept_index, kept_keys, kept_values, target)
+    mine, send, kept = pack(core, queries, positions, kept_index)
+    other = lax.ppermute(send, "core", swap)
+    target, q, pos, kept_keys, kept_values = attend(core, mine, other, kept, history_keys, history_values)
+    expo, over, z = start(core, q, pos, kept, kept_keys, kept_values, target)
 
     def exchange(chunks):
         return lax.all_to_all(chunks, "chip", 0, 0, tiled=True)

time: 175 us -> 175 us (level)
  Pallas kernels: 82.1 us -> 38 us
  blocking collectives: 82.9 us -> 123 us
  starting transfers between devices: 9.66 us -> 14.4 us
    pallas_call x1, Pallas kernels: 68 us -> 24.8 us  [attend(): pl.pallas_call(attend_kernel, grid_spec=pltpu.PrefetchScalarGridSpec(num_...]
    all_to_all x4, blocking collectives: 65.3 us -> 104 us  [exchange(): return lax.all_to_all(chunks, 'chip', 0, 0, tiled=True)]
    ppermute x1, starting transfers between devices: 8.16 us -> 12.9 us  [local(): got = lax.ppermute(send, 'core', swap)]
where the time goes in v5:
time: 175 us; the launch traced here: 177 us
  blocking collectives  123 us (70%)
  Pallas kernels  38 us (22%)
  starting transfers between devices  14.4 us (8%)
    all_to_all x4, blocking collectives, exchange(): return lax.all_to_all(chunks, 'chip', 0, 0, tiled=True)  104 us
    pallas_call x1, Pallas kernels, attend(): pl.pallas_call(attend_kernel, grid_spec=pltpu.PrefetchScalarGridSpec(num_...  24.8 us
    all_to_all x1, blocking collectives, local(): sums = lax.all_to_all(sums, ('head', 'chip', 'core'), 0, 0, tiled=True)  19.1 us
    ppermute x1, starting transfers between devices, local(): got = lax.ppermute(send, 'core', swap)  12.9 us
    pallas_call x1, Pallas kernels, start(): pl.pallas_call(start_kernel, grid_spec=pltpu.PrefetchScalarGridSpec(num_s...  7.19 us
    pallas_call x2, Pallas kernels, with_weights(): pl.pallas_call(kernel, in_specs=[whole(vec.shape), whole(over.shape), who...  3.85 us
  transfers between devices with their start and end apart: 2, of which 1 were waited for; matrix products, arithmetic and copies ran while one was open for 0% of the time, Pallas kernels for 1%

profile of v5, /device:TPU:1, one launch (start us, length us, event | category | flops | bytes accessed | tf_op | source)
XLA Modules:
  0.0 176.8 jit_solution(7301214608630838470)
XLA Ops:
  0.0 1.0 pack.1
  1.0 1.5 collective-permute-start
  2.5 1.2 collective-permute-done.other_ref
  3.7 24.8 %attend.1 = (f32[1024,128]{1,0:T(8,128)S(1)}, bf16[1024,128]{1,0:T(8,128)(2,1)S(1)}, f32[8,128]{1,0:T(8,128)S(1)}, bf16[2048,128]{1,0:T(8,128)(2,1)S(1)}, bf16[2048,128]{1,0:T(8,128)(2,1)S(1)}) custom-call(s32[1]{0:T(128)} %bitcast.core.refs_0_, f32[520,128]{1,0:T(8,128)S(1)} %get-tuple-element.24.mine_ref, f32[520,128]{1,0:T(8,128)S(1)} %collective-permute-done.other_ref, ...), custom_call_target="tpu_custom_call" | custom-call | tf_op jit(solution)/shard_map/attend/pallas_call | solution.py:217
  28.5 7.2 %start.1 = (bf16[1024,2048]{1,0:T(8,128)(2,1)S(1)}, f32[8,1024]{1,0:T(8,128)S(1)}, f32[16,128,128]{2,1,0:T(8,128)S(1)}) custom-call(s32[1]{0:T(128)} %bitcast.core.refs_0_, bf16[1024,128]{1,0:T(8,128)(2,1)S(1)} %get-tuple-element.27.q_ref, f32[8,128]{1,0:T(8,128)S(1)} %get-tuple-element.28.pos_ref, s32[2,2048]{1,0:T(2,128)S(1)} %get-tuple-element.26.kept_ref, ...), custom_call_target="tpu_custom_call" | custom-call | tf_op jit(solution)/shard_map/start/pallas_call | solution.py:290
  35.7 59.1 %all_to_all.25.parts_ref = f32[16,128,128]{2,1,0:T(8,128)S(1)} all-to-all(f32[16,128,128]{2,1,0:T(8,128)S(1)} %get-tuple-element.32), channel_id=1, replica_groups=mesh['head'=4,'chip'=16,'core'=2] {'chip'}, dimensions={0} | all-to-all | bytes 2097152 | tf_op jit(solution)/shard_map/all_to_all | solution.py:474
  94.8 0.1 fold.1
  94.9 14.5 %all_to_all.26.vec_ref = f32[16,128,128]{2,1,0:T(8,128)S(1)} all-to-all(f32[16,128,128]{2,1,0:T(8,128)S(1)} %get-tuple-element.33), channel_id=1, replica_groups=mesh['head'=4,'chip'=16,'core'=2] {'chip'}, dimensions={0} | all-to-all | bytes 2097152 | tf_op jit(solution)/shard_map/all_to_all | solution.py:474
  109.4 2.4 %normal.1 = f32[16,128,128]{2,1,0:T(8,128)S(1)} custom-call(f32[16,128,128]{2,1,0:T(8,128)S(1)} %all_to_all.26.vec_ref, f32[8,1024]{1,0:T(8,128)S(1)} %get-tuple-element.34.over_ref, bf16[1024,2048]{1,0:T(8,128)(2,1)S(1)} %get-tuple-element.35.e_ref), custom_call_target="tpu_custom_call" | custom-call | tf_op jit(solution)/shard_map/normal/pallas_call | solution.py:354
  111.8 14.5 %all_to_all.27.refs_1_ = f32[16,128,128]{2,1,0:T(8,128)S(1)} all-to-all(f32[16,128,128]{2,1,0:T(8,128)S(1)} %normal.1), channel_id=1, replica_groups=mesh['head'=4,'chip'=16,'core'=2] {'chip'}, dimensions={0} | all-to-all | bytes 2097152 | tf_op jit(solution)/shard_map/all_to_all | solution.py:474
  126.3 0.2 fold_image.1
  126.5 15.9 %all_to_all.28.vec_ref = f32[16,128,128]{2,1,0:T(8,128)S(1)} all-to-all(f32[16,128,128]{2,1,0:T(8,128)S(1)} %get-tuple-element.37), channel_id=1, replica_groups=mesh['head'=4,'chip'=16,'core'=2] {'chip'}, dimensions={0} | all-to-all | bytes 2097152 | tf_op jit(solution)/shard_map/all_to_all | solution.py:474
  142.4 12.9 %collective-permute-start.1 = (f32[2,64,128]{2,1,0:T(8,128)S(1)}, f32[2,64,128]{2,1,0:T(8,128)S(1)}, u32[]{:S(2)}, u32[]{:S(2)}) collective-permute-start(f32[2,64,128]{2,1,0:T(8,128)S(1)} %get-tuple-element.42), channel_id=1, source_target_pairs={{0,1},{1,0},{2,3},{3,2},{4,5},{5,4},{6,7},{7,6},{8,9},{9,8},{10,11... | collective-permute-start | bytes 196616 | tf_op jit(solution)/shard_map/ppermute | solution.py:482
  155.3 1.4 square.1
  156.7 19.1 %all_to_all.29.refs_1_ = f32[128,1,128]{2,1,0:T(1,128)S(1)} all-to-all(f32[128,1,128]{2,1,0:T(1,128)S(1)} %square.1), channel_id=1, replica_groups=mesh['head'=4,'chip'=16,'core'=2] {'head','chip','core'}, dimensions={0} | all-to-all | bytes 131072 | tf_op jit(solution)/shard_map/all_to_all | solution.py:484
  175.9 0.0 collective-permute-done.1.refs_3_
  175.9 0.9 finish.1
Async XLA Ops:
  1.0 2.7 %collective-permute-start = (f32[520,128]{1,0:T(8,128)S(1)}, f32[520,128]{1,0:T(8,128)S(1)}, u32[]{:S(2)}, u32[]{:S(2)}) collective-permute-start(f32[520,128]{1,0:T(8,128)S(1)} %get-tuple-element.25), channel_id=1, source_target_pairs={{0,1},{1,0},{2,3},{3,2},{4,5},{5,4},{6,7},{7,6},{8,9},{9,8},{10,11... | collective-permute-start | bytes 798728 | tf_op jit(solution)/shard_map/ppermute | solution.py:469
  142.4 33.5 %collective-permute-start.1 = (f32[2,64,128]{2,1,0:T(8,128)S(1)}, f32[2,64,128]{2,1,0:T(8,128)S(1)}, u32[]{:S(2)}, u32[]{:S(2)}) collective-permute-start(f32[2,64,128]{2,1,0:T(8,128)S(1)} %get-tuple-element.42), channel_id=1, source_target_pairs={{0,1},{1,0},{2,3},{3,2},{4,5},{5,4},{6,7},{7,6},{8,9},{9,8},{10,11... | collective-permute-start | bytes 196616 | tf_op jit(solution)/shard_map/ppermute | solution.py:482

commit v6 on v5

--- a/solution.py
+++ b/solution.py
@@ -267,6 +267,7 @@
 def start_kernel(core, q_ref, pos_ref, kept_ref, kk_ref, kv_ref, t_ref, e_ref, over_ref, z_ref, low_ref, two_ref):
     kept = kept_ref[pl.ds(core[0], 1), :]
     cols = columns_of(pos_ref[...])
+    values = jnp.concatenate([kv_ref[...], kv_ref[...]], axis=0)
     for tile in range(e_ref.shape[0] // ROWS):
         here = pl.ds(tile * ROWS, ROWS)
         scores = dot(q_ref[here, :], kk_ref[...], NT) * SCALE
@@ -277,7 +278,7 @@
         high, low = halves(expo)
         e_ref[here, :] = high
         low_ref[here, :] = low
-        gap = t_ref[here, :] - (dot(high, kv_ref[...]) + dot(low, kv_ref[...])) * over
+        gap = t_ref[here, :] - dot(jnp.concatenate([high, low], axis=1), values) * over
         over_ref[:, here] = jnp.transpose(jnp.broadcast_to(over, (ROWS, LANES)))[:8, :]
         two_ref[:, here] = stacked(jnp.transpose(gap * over))
     put_chunks(z_ref, pulled(two_ref[...], e_ref[...]) + dot(two_ref[:HD, :], low_ref[...]))

time: 175 us -> 174 us (level)
  starting transfers between devices: 14.4 us -> 11.8 us
  blocking collectives: 123 us -> 125 us
    ppermute x1, starting transfers between devices: 12.9 us -> 10.3 us  [local(): got = lax.ppermute(send, 'core', swap)]
where the time goes in v6:
time: 174 us; the launch traced here: 176 us
  blocking collectives  125 us (72%)
  Pallas kernels  37.7 us (22%)
  starting transfers between devices  11.8 us (7%)
    all_to_all x4, blocking collectives, exchange(): return lax.all_to_all(chunks, 'chip', 0, 0, tiled=True)  105 us
    pallas_call x1, Pallas kernels, attend(): pl.pallas_call(attend_kernel, grid_spec=pltpu.PrefetchScalarGridSpec(num_...  24.8 us
    all_to_all x1, blocking collectives, local(): sums = lax.all_to_all(sums, ('head', 'chip', 'core'), 0, 0, tiled=True)  19.9 us
    ppermute x1, starting transfers between devices, local(): got = lax.ppermute(send, 'core', swap)  10.3 us
    pallas_call x1, Pallas kernels, start(): pl.pallas_call(start_kernel, grid_spec=pltpu.PrefetchScalarGridSpec(num_s...  6.83 us
    pallas_call x2, Pallas kernels, with_weights(): pl.pallas_call(kernel, in_specs=[whole(vec.shape), whole(over.shape), who...  3.85 us
  transfers between devices with their start and end apart: 2, of which 1 were waited for; matrix products, arithmetic and copies ran while one was open for 0% of the time, Pallas kernels for 1%

profile of v6, /device:TPU:1, one launch (start us, length us, event | category | flops | bytes accessed | tf_op | source)
XLA Modules:
  0.0 175.6 jit_solution(2180669342869252039)
XLA Ops:
  0.0 1.0 pack.1
  1.0 1.5 collective-permute-start
  2.5 1.2 collective-permute-done.other_ref
  3.7 24.8 %attend.1 = (f32[1024,128]{1,0:T(8,128)S(1)}, bf16[1024,128]{1,0:T(8,128)(2,1)S(1)}, f32[8,128]{1,0:T(8,128)S(1)}, bf16[2048,128]{1,0:T(8,128)(2,1)S(1)}, bf16[2048,128]{1,0:T(8,128)(2,1)S(1)}) custom-call(s32[1]{0:T(128)} %bitcast.core.refs_0_, f32[520,128]{1,0:T(8,128)S(1)} %get-tuple-element.24.mine_ref, f32[520,128]{1,0:T(8,128)S(1)} %collective-permute-done.other_ref, ...), custom_call_target="tpu_custom_call" | custom-call | tf_op jit(solution)/shard_map/attend/pallas_call | solution.py:217
  28.5 6.8 %start.1 = (bf16[1024,2048]{1,0:T(8,128)(2,1)S(1)}, f32[8,1024]{1,0:T(8,128)S(1)}, f32[16,128,128]{2,1,0:T(8,128)S(1)}) custom-call(s32[1]{0:T(128)} %bitcast.core.refs_0_, bf16[1024,128]{1,0:T(8,128)(2,1)S(1)} %get-tuple-element.27.q_ref, f32[8,128]{1,0:T(8,128)S(1)} %get-tuple-element.28.pos_ref, s32[2,2048]{1,0:T(2,128)S(1)} %get-tuple-element.26.kept_ref, ...), custom_call_target="tpu_custom_call" | custom-call | tf_op jit(solution)/shard_map/start/pallas_call | solution.py:291
  35.3 61.5 %all_to_all.25.parts_ref = f32[16,128,128]{2,1,0:T(8,128)S(1)} all-to-all(f32[16,128,128]{2,1,0:T(8,128)S(1)} %get-tuple-element.32), channel_id=1, replica_groups=mesh['head'=4,'chip'=16,'core'=2] {'chip'}, dimensions={0} | all-to-all | bytes 2097152 | tf_op jit(solution)/shard_map/all_to_all | solution.py:475
  96.8 0.1 fold.1
  97.0 14.6 %all_to_all.26.vec_ref = f32[16,128,128]{2,1,0:T(8,128)S(1)} all-to-all(f32[16,128,128]{2,1,0:T(8,128)S(1)} %get-tuple-element.33), channel_id=1, replica_groups=mesh['head'=4,'chip'=16,'core'=2] {'chip'}, dimensions={0} | all-to-all | bytes 2097152 | tf_op jit(solution)/shard_map/all_to_all | solution.py:475
  111.6 2.4 %normal.1 = f32[16,128,128]{2,1,0:T(8,128)S(1)} custom-call(f32[16,128,128]{2,1,0:T(8,128)S(1)} %all_to_all.26.vec_ref, f32[8,1024]{1,0:T(8,128)S(1)} %get-tuple-element.34.over_ref, bf16[1024,2048]{1,0:T(8,128)(2,1)S(1)} %get-tuple-element.35.e_ref), custom_call_target="tpu_custom_call" | custom-call | tf_op jit(solution)/shard_map/normal/pallas_call | solution.py:355
  114.0 14.5 %all_to_all.27.refs_1_ = f32[16,128,128]{2,1,0:T(8,128)S(1)} all-to-all(f32[16,128,128]{2,1,0:T(8,128)S(1)} %normal.1), channel_id=1, replica_groups=mesh['head'=4,'chip'=16,'core'=2] {'chip'}, dimensions={0} | all-to-all | bytes 2097152 | tf_op jit(solution)/shard_map/all_to_all | solution.py:475
  128.4 0.2 fold_image.1
  128.6 14.5 %all_to_all.28.vec_ref = f32[16,128,128]{2,1,0:T(8,128)S(1)} all-to-all(f32[16,128,128]{2,1,0:T(8,128)S(1)} %get-tuple-element.37), channel_id=1, replica_groups=mesh['head'=4,'chip'=16,'core'=2] {'chip'}, dimensions={0} | all-to-all | bytes 2097152 | tf_op jit(solution)/shard_map/all_to_all | solution.py:475
  143.1 10.3 %collective-permute-start.1 = (f32[2,64,128]{2,1,0:T(8,128)S(1)}, f32[2,64,128]{2,1,0:T(8,128)S(1)}, u32[]{:S(2)}, u32[]{:S(2)}) collective-permute-start(f32[2,64,128]{2,1,0:T(8,128)S(1)} %get-tuple-element.42), channel_id=1, source_target_pairs={{0,1},{1,0},{2,3},{3,2},{4,5},{5,4},{6,7},{7,6},{8,9},{9,8},{10,11... | collective-permute-start | bytes 196616 | tf_op jit(solution)/shard_map/ppermute | solution.py:483
  153.4 1.4 square.1
  154.8 19.9 %all_to_all.29.refs_1_ = f32[128,1,128]{2,1,0:T(1,128)S(1)} all-to-all(f32[128,1,128]{2,1,0:T(1,128)S(1)} %square.1), channel_id=1, replica_groups=mesh['head'=4,'chip'=16,'core'=2] {'head','chip','core'}, dimensions={0} | all-to-all | bytes 131072 | tf_op jit(solution)/shard_map/all_to_all | solution.py:485
  174.7 0.0 collective-permute-done.1.refs_3_
  174.7 0.9 finish.1
Async XLA Ops:
  1.0 2.7 %collective-permute-start = (f32[520,128]{1,0:T(8,128)S(1)}, f32[520,128]{1,0:T(8,128)S(1)}, u32[]{:S(2)}, u32[]{:S(2)}) collective-permute-start(f32[520,128]{1,0:T(8,128)S(1)} %get-tuple-element.25), channel_id=1, source_target_pairs={{0,1},{1,0},{2,3},{3,2},{4,5},{5,4},{6,7},{7,6},{8,9},{9,8},{10,11... | collective-permute-start | bytes 798728 | tf_op jit(solution)/shard_map/ppermute | solution.py:470
  143.1 31.6 %collective-permute-start.1 = (f32[2,64,128]{2,1,0:T(8,128)S(1)}, f32[2,64,128]{2,1,0:T(8,128)S(1)}, u32[]{:S(2)}, u32[]{:S(2)}) collective-permute-start(f32[2,64,128]{2,1,0:T(8,128)S(1)} %get-tuple-element.42), channel_id=1, source_target_pairs={{0,1},{1,0},{2,3},{3,2},{4,5},{5,4},{6,7},{7,6},{8,9},{9,8},{10,11... | collective-permute-start | bytes 196616 | tf_op jit(solution)/shard_map/ppermute | solution.py:483

commit v7 on v6

--- a/solution.py
+++ b/solution.py
@@ -189,20 +189,24 @@
             def _(masked=masked, running=running):
                 go(masked, running)
 
-    @pl.when((step == steps - 1) & jnp.logical_not(jnp.max(jnp.max(acc_ref[:, HD : HD + 1], axis=0, keepdims=True)) <= LIMIT))
+    @pl.when(step == steps - 1)
     def _():
-        m_ref[...] = jnp.full(m_ref.shape, -jnp.inf, f32)
-        acc_ref[...] = jnp.zeros(acc_ref.shape, f32)
-
-        def block(j, carry):
-            fetch(j, 0)
-            arrive(j, 0)
-            load(0)
-            for tile in range(tiles):
-                tile_now(tile, 0, j * BLOCK, True, True)
-            return carry
-
-        lax.fori_loop(0, steps, block, 0)
+        largest = jnp.max(jnp.max(acc_ref[:, HD : HD + 1], axis=0, keepdims=True))
+
+        @pl.when(jnp.logical_not(largest <= LIMIT))
+        def _():
+            m_ref[...] = jnp.full(m_ref.shape, -jnp.inf, f32)
+            acc_ref[...] = jnp.zeros(acc_ref.shape, f32)
+
+            def block(j, carry):
+                fetch(j, 0)
+                arrive(j, 0)
+                load(0)
+                for tile in range(tiles):
+                    tile_now(tile, 0, j * BLOCK, True, True)
+                return carry
+
+            lax.fori_loop(0, steps, block, 0)
 
     @pl.when(step == steps - 1)
     def _():

time: 174 us -> 174 us (level)
  blocking collectives: 125 us -> 130 us
  starting transfers between devices: 11.8 us -> 7.92 us
    all_to_all x4, blocking collectives: 105 us -> 111 us  [exchange(): return lax.all_to_all(chunks, 'chip', 0, 0, tiled=True)]
    ppermute x1, starting transfers between devices: 10.3 us -> 6.42 us  [local(): got = lax.ppermute(send, 'core', swap)]
where the time goes in v7:
time: 174 us; the launch traced here: 176 us
  blocking collectives  130 us (75%)
  Pallas kernels  37.1 us (21%)
  starting transfers between devices  7.92 us (5%)
    all_to_all x4, blocking collectives, exchange(): return lax.all_to_all(chunks, 'chip', 0, 0, tiled=True)  111 us
    pallas_call x1, Pallas kernels, attend(): pl.pallas_call(attend_kernel, grid_spec=pltpu.PrefetchScalarGridSpec(num_...  24.2 us
    all_to_all x1, blocking collectives, local(): sums = lax.all_to_all(sums, ('head', 'chip', 'core'), 0, 0, tiled=True)  18.8 us
    pallas_call x1, Pallas kernels, start(): pl.pallas_call(start_kernel, grid_spec=pltpu.PrefetchScalarGridSpec(num_s...  6.84 us
    ppermute x1, starting transfers between devices, local(): got = lax.ppermute(send, 'core', swap)  6.42 us
    pallas_call x2, Pallas kernels, with_weights(): pl.pallas_call(kernel, in_specs=[whole(vec.shape), whole(over.shape), who...  3.85 us
  transfers between devices with their start and end apart: 2, of which 1 were waited for; matrix products, arithmetic and copies ran while one was open for 0% of the time, Pallas kernels for 1%

profile of v7, /device:TPU:1, one launch (start us, length us, event | category | flops | bytes accessed | tf_op | source)
XLA Modules:
  0.0 176.0 jit_solution(17779009337042164268)
XLA Ops:
  0.0 1.0 pack.1
  1.0 1.5 collective-permute-start
  2.5 1.2 collective-permute-done.other_ref
  3.7 24.2 %attend.1 = (f32[1024,128]{1,0:T(8,128)S(1)}, bf16[1024,128]{1,0:T(8,128)(2,1)S(1)}, f32[8,128]{1,0:T(8,128)S(1)}, bf16[2048,128]{1,0:T(8,128)(2,1)S(1)}, bf16[2048,128]{1,0:T(8,128)(2,1)S(1)}) custom-call(s32[1]{0:T(128)} %bitcast.core.refs_0_, f32[520,128]{1,0:T(8,128)S(1)} %get-tuple-element.24.mine_ref, f32[520,128]{1,0:T(8,128)S(1)} %collective-permute-done.other_ref, ...), custom_call_target="tpu_custom_call" | custom-call | tf_op jit(solution)/shard_map/attend/pallas_call | solution.py:221
  27.9 6.8 %start.1 = (bf16[1024,2048]{1,0:T(8,128)(2,1)S(1)}, f32[8,1024]{1,0:T(8,128)S(1)}, f32[16,128,128]{2,1,0:T(8,128)S(1)}) custom-call(s32[1]{0:T(128)} %bitcast.core.refs_0_, bf16[1024,128]{1,0:T(8,128)(2,1)S(1)} %get-tuple-element.27.q_ref, f32[8,128]{1,0:T(8,128)S(1)} %get-tuple-element.28.pos_ref, s32[2,2048]{1,0:T(2,128)S(1)} %get-tuple-element.26.kept_ref, ...), custom_call_target="tpu_custom_call" | custom-call | tf_op jit(solution)/shard_map/start/pallas_call | solution.py:295
  34.7 64.3 %all_to_all.25.parts_ref = f32[16,128,128]{2,1,0:T(8,128)S(1)} all-to-all(f32[16,128,128]{2,1,0:T(8,128)S(1)} %get-tuple-element.32), channel_id=1, replica_groups=mesh['head'=4,'chip'=16,'core'=2] {'chip'}, dimensions={0} | all-to-all | bytes 2097152 | tf_op jit(solution)/shard_map/all_to_all | solution.py:479
  99.1 0.1 fold.1
  99.2 16.0 %all_to_all.26.vec_ref = f32[16,128,128]{2,1,0:T(8,128)S(1)} all-to-all(f32[16,128,128]{2,1,0:T(8,128)S(1)} %get-tuple-element.33), channel_id=1, replica_groups=mesh['head'=4,'chip'=16,'core'=2] {'chip'}, dimensions={0} | all-to-all | bytes 2097152 | tf_op jit(solution)/shard_map/all_to_all | solution.py:479
  115.2 2.4 %normal.1 = f32[16,128,128]{2,1,0:T(8,128)S(1)} custom-call(f32[16,128,128]{2,1,0:T(8,128)S(1)} %all_to_all.26.vec_ref, f32[8,1024]{1,0:T(8,128)S(1)} %get-tuple-element.34.over_ref, bf16[1024,2048]{1,0:T(8,128)(2,1)S(1)} %get-tuple-element.35.e_ref), custom_call_target="tpu_custom_call" | custom-call | tf_op jit(solution)/shard_map/normal/pallas_call | solution.py:359
  117.6 15.9 %all_to_all.27.refs_1_ = f32[16,128,128]{2,1,0:T(8,128)S(1)} all-to-all(f32[16,128,128]{2,1,0:T(8,128)S(1)} %normal.1), channel_id=1, replica_groups=mesh['head'=4,'chip'=16,'core'=2] {'chip'}, dimensions={0} | all-to-all | bytes 2097152 | tf_op jit(solution)/shard_map/all_to_all | solution.py:479
  133.5 0.2 fold_image.1
  133.7 14.7 %all_to_all.28.vec_ref = f32[16,128,128]{2,1,0:T(8,128)S(1)} all-to-all(f32[16,128,128]{2,1,0:T(8,128)S(1)} %get-tuple-element.37), channel_id=1, replica_groups=mesh['head'=4,'chip'=16,'core'=2] {'chip'}, dimensions={0} | all-to-all | bytes 2097152 | tf_op jit(solution)/shard_map/all_to_all | solution.py:479
  148.5 6.4 %collective-permute-start.1 = (f32[2,64,128]{2,1,0:T(8,128)S(1)}, f32[2,64,128]{2,1,0:T(8,128)S(1)}, u32[]{:S(2)}, u32[]{:S(2)}) collective-permute-start(f32[2,64,128]{2,1,0:T(8,128)S(1)} %get-tuple-element.42), channel_id=1, source_target_pairs={{0,1},{1,0},{2,3},{3,2},{4,5},{5,4},{6,7},{7,6},{8,9},{9,8},{10,11... | collective-permute-start | bytes 196616 | tf_op jit(solution)/shard_map/ppermute | solution.py:487
  154.9 1.4 square.1
  156.3 18.8 %all_to_all.29.refs_1_ = f32[128,1,128]{2,1,0:T(1,128)S(1)} all-to-all(f32[128,1,128]{2,1,0:T(1,128)S(1)} %square.1), channel_id=1, replica_groups=mesh['head'=4,'chip'=16,'core'=2] {'head','chip','core'}, dimensions={0} | all-to-all | bytes 131072 | tf_op jit(solution)/shard_map/all_to_all | solution.py:489
  175.1 0.0 collective-permute-done.1.refs_3_
  175.1 0.9 finish.1
Async XLA Ops:
  1.0 2.7 %collective-permute-start = (f32[520,128]{1,0:T(8,128)S(1)}, f32[520,128]{1,0:T(8,128)S(1)}, u32[]{:S(2)}, u32[]{:S(2)}) collective-permute-start(f32[520,128]{1,0:T(8,128)S(1)} %get-tuple-element.25), channel_id=1, source_target_pairs={{0,1},{1,0},{2,3},{3,2},{4,5},{5,4},{6,7},{7,6},{8,9},{9,8},{10,11... | collective-permute-start | bytes 798728 | tf_op jit(solution)/shard_map/ppermute | solution.py:474
  148.5 26.6 %collective-permute-start.1 = (f32[2,64,128]{2,1,0:T(8,128)S(1)}, f32[2,64,128]{2,1,0:T(8,128)S(1)}, u32[]{:S(2)}, u32[]{:S(2)}) collective-permute-start(f32[2,64,128]{2,1,0:T(8,128)S(1)} %get-tuple-element.42), channel_id=1, source_target_pairs={{0,1},{1,0},{2,3},{3,2},{4,5},{5,4},{6,7},{7,6},{8,9},{9,8},{10,11... | collective-permute-start | bytes 196616 | tf_op jit(solution)/shard_map/ppermute | solution.py:487
